TPU v7x, 512 devices: a whole 4x8x8 slice. The times are simulated.
512 devices in a mesh: tile: 16 (over x_hi, z), sect: 4 (over x_lo, core), emu: 8 (over y).
Axes of the slice: x: 4 (x_hi: 2, x_lo: 2; x = x_hi * 2 + x_lo), y: 8, z: 8, core: 2. Of those that a mesh axis runs over, the one named last changes fastest.
Arguments:
- state: float32 [8, 16, 256, 512], P(None, None, 'tile', ('sect', 'emu')), may hold values from -6 to 6
- winds: float32 [2, 16, 256, 512], P(None, None, 'tile', ('sect', 'emu')), may hold values from -0.5 to 0.5
- regime_table: int32 [16, 32, 256, 1], P('tile', ('sect', 'emu')), may hold values from 0 to 3; in each aligned block of 256 rows (0 to 255, 256 to 511, ..., all dimensions but the last counted through in order) at most 128 rows name the same one
- emu_lift: bfloat16 [4, 128, 8], P('sect'), may hold values from -2 to 2
- emu_conv: bfloat16 [4, 4, 3, 128, 128], P('sect'), may hold values from -0.3125 to 0.3125
- emu_output: bfloat16 [4, 8, 128], P('sect'), may hold values from -0.5 to 0.5
Outputs:
- final_state: float32 [8, 16, 256, 512], P(None, None, 'tile', ('sect', 'emu'))
Inputs may be any that keep to these rules, and one draw needn't show every extreme that they name: `regime_table`: among the columns of one device (one block of the table), no regime is named more than 128 times, and in every draw some block names one regime exactly 128 times.
All inputs are finite; a program needn't handle non-finite values.
Results may differ from a plain program's by a relative error of at most 0.025.
Values may be sent and summed in bfloat16 or wider, within the bound.
A program may use at most 128 MiB of HBM per device.

v0:
```python
import functools

import jax
import jax.numpy as jnp
from jax import lax
from jax.experimental import pallas as pl
from jax.experimental.pallas import tpu as pltpu
from jax.sharding import PartitionSpec as P

MESH = pl.DeviceIdType.MESH
STEPS = 2
SIDE = 16
LANES = 128
VARS = 8
LEVELS = 16
REGIMES = 4
LAYERS = 4
TILE = 32
TILES = 11
SLOTS = TILES * TILE
PAD_SLOTS = 384
X0, Y0 = 6, 8
PAD_X, PAD_Y = 28, 32
DIRECTIONS = ((1, 0), (-1, 0), (0, 1), (0, -1), (1, 1), (1, -1), (-1, 1), (-1, -1))
BF16 = jnp.bfloat16
F32 = jnp.float32


def dot(a, b):
    return jnp.dot(a, b, preferred_element_type=F32)


def dot_nt(a, b):
    return lax.dot_general(a, b, (((1,), (1,)), ((), ())), preferred_element_type=F32)


def iota(shape, dim):
    return lax.broadcasted_iota(jnp.int32, shape, dim)


def field_rows(dx, dy):
    return 96 if dy == 0 else 128 if dx == 0 else 32


def wind_rows(dx, dy):
    return 16 if dx and dy else 32


def sent_box(dx, dy):
    if dx and dy:
        xs = slice(X0 + 12, X0 + 16) if dx > 0 else slice(X0, X0 + 4)
    elif dx:
        xs = slice(X0 + 10, X0 + 16) if dx > 0 else slice(X0, X0 + 6)
    else:
        xs = slice(X0, X0 + SIDE)
    ys = slice(Y0, Y0 + SIDE)
    if dy:
        ys = slice(Y0 + 8, Y0 + 16) if dy > 0 else slice(Y0, Y0 + 8)
    return xs, ys


def landing_box(dx, dy):
    xs, ys = sent_box(dx, dy)
    return (
        slice(xs.start - SIDE * dx, xs.stop - SIDE * dx),
        slice(ys.start - SIDE * dy, ys.stop - SIDE * dy),
    )


def wind_groups(dx, dy):
    ys = sent_box(dx, dy)[1]
    if dx == 0:
        return [(slice(X0 + 4 * g, X0 + 4 * g + 4), ys) for g in range(4)]
    base = X0 + 8 if dx > 0 else X0
    return [(slice(base + 2 * g, base + 2 * g + 2), ys) for g in range(4)]


def local_tendency(src, east, north, flux, xs, ys):
    nx, ny = xs.stop - xs.start, ys.stop - ys.start

    def face_flux(speed, before, center, after, beyond):
        both = 2.0 * (center + after)
        up = jnp.maximum(speed, 0.0)
        down = jnp.minimum(speed, 0.0)
        return up * (both + 3.0 * center - before) + down * (both + 3.0 * after - beyond)

    along_x = src[xs.start - 2 : xs.stop + 2, ys, :]
    flux_x = face_flux(
        east[xs.start - 1 : xs.stop, ys, :],
        along_x[0 : nx + 1],
        along_x[1 : nx + 2],
        along_x[2 : nx + 3],
        along_x[3 : nx + 4],
    )
    total = flux_x[:nx] - flux_x[1:]
    faces = slice(ys.start - 1, ys.stop)
    flux[0:nx, 0 : ny + 1, :] = face_flux(
        north[xs, faces, :],
        src[xs, faces.start - 1 : faces.stop - 1, :],
        src[xs, faces, :],
        src[xs, faces.start + 1 : faces.stop + 1, :],
        src[xs, faces.start + 2 : faces.stop + 2, :],
    )
    return total + (flux[0:nx, 0:ny, :] - flux[0:nx, 1 : ny + 1, :])


def kernel(
    state_ref, wind_ref, regime_ref, small_ref, conv_ref, out_ref,
    field, first, second, east, north, flux,
    send_x, recv_x, send_y, recv_y, send_c, recv_c,
    conv, small, lift_map, out_map, spread, pick, unpick, ordered, answers,
    halo_send, halo_recv, weight_send, weight_recv, small_send, small_recv, own_sem,
):
    count_tile, count_sect, count_emu = (lax.axis_size(n) for n in ("tile", "sect", "emu"))
    tile, sect, emu = (lax.axis_index(n) for n in ("tile", "sect", "emu"))
    along_y = sect * count_emu + emu
    total_y = count_sect * count_emu

    def neighbour(dx, dy):
        y = lax.rem(along_y + (dy + total_y), total_y)
        return (lax.rem(tile + (dx + count_tile), count_tile), y // count_emu, lax.rem(y, count_emu))

    half = count_tile // 2
    far_tile = lax.rem(tile + half, count_tile)
    core, chip = lax.rem(sect, 2), sect // 2
    partners = (
        (tile, chip * 2 + (1 - core), emu),
        (tile, (1 - chip) * 2 + core, emu),
        (far_tile, (1 - chip) * 2 + (1 - core), emu),
    )
    neighbours = [neighbour(dx, dy) for dx, dy in DIRECTIONS]

    barrier = pltpu.get_barrier_semaphore()
    for device in (*neighbours, *partners):
        pl.semaphore_signal(barrier, inc=1, device_id=device, device_id_type=MESH)

    own_copies = [
        pltpu.make_async_copy(conv_ref, conv.at[sect], own_sem.at[0]),
        pltpu.make_async_copy(small_ref, small.at[sect], own_sem.at[1]),
    ]
    for copy in own_copies:
        copy.start()

    row, column = iota((LANES, 8 * LANES), 0), iota((LANES, 8 * LANES), 1)
    group, part = column // (2 * LANES), (column // LANES) % 2
    chosen = (row // LEVELS == part * 4 + group) & (row % LEVELS == column % LEVELS)
    spread[...] = jnp.where(chosen, 1.0, 0.0).astype(BF16)
    wide = dot(wind_ref[...], spread[...])
    for g in range(4):
        at = (slice(X0 + 4 * g, X0 + 4 * g + 4), slice(Y0, Y0 + SIDE), slice(None))
        east[at] = wide[:, 256 * g : 256 * g + 128].reshape(4, SIDE, LANES)
        north[at] = wide[:, 256 * g + 128 : 256 * g + 256].reshape(4, SIDE, LANES)
    field[X0 : X0 + SIDE, Y0 : Y0 + SIDE, :] = state_ref[...].reshape(SIDE, SIDE, LANES)

    def buffers(step, k):
        dx, dy = DIRECTIONS[k]
        if dy == 0:
            return send_x.at[step, k], recv_x.at[step, k]
        if dx == 0:
            return send_y.at[step, k - 2], recv_y.at[step, k - 2]
        return send_c.at[step, k - 4], recv_c.at[step, k - 4]

    def halo_copy(step, k):
        sent, received = buffers(step, k)
        rows = field_rows(*DIRECTIONS[k]) + (wind_rows(*DIRECTIONS[k]) if step == 0 else 0)
        return pltpu.make_async_remote_copy(
            src_ref=sent.at[0:rows],
            dst_ref=received.at[0:rows],
            send_sem=halo_send.at[step, k],
            recv_sem=halo_recv.at[step, k],
            device_id=neighbours[k],
            device_id_type=MESH,
        )

    def pack(step):
        for k, (dx, dy) in enumerate(DIRECTIONS):
            sent, _ = buffers(step, k)
            xs, ys = sent_box(dx, dy)
            rows = field_rows(dx, dy)
            sent[0:rows, :] = field[xs, ys, :].reshape(rows, LANES).astype(BF16)
            if step == 0:
                more = wind_rows(dx, dy)
                quarter = iota((more, LANES), 1) // LEVELS
                packed = jnp.zeros((more, LANES), F32)
                for c, winds in enumerate((east, north)):
                    for g, (gx, gy) in enumerate(wind_groups(dx, dy)):
                        if dx and dy and g // 2 != (1 if dx > 0 else 0):
                            continue
                        piece = winds[gx, gy, :].reshape(more, LANES)
                        packed = jnp.where(quarter == c * 4 + g, piece, packed)
                sent[rows : rows + more, :] = packed.astype(BF16)

    def unpack(step):
        for k, (dx, dy) in enumerate(DIRECTIONS):
            _, received = buffers(step, k)
            xs, ys = landing_box(dx, dy)
            rows = field_rows(dx, dy)
            nx, ny = xs.stop - xs.start, ys.stop - ys.start
            field[xs, ys, :] = received[0:rows, :].astype(F32).reshape(nx, ny, LANES)
            if step == 0:
                more = wind_rows(dx, dy)
                wide = dot(received[rows : rows + more, :], spread[...])
                for g, (gx, gy) in enumerate(wind_groups(dx, dy)):
                    if dx and dy and g // 2 != (1 if dx > 0 else 0):
                        continue
                    x_from, x_to = gx.start - SIDE * dx, gx.stop - SIDE * dx
                    if x_from < 0 or x_to > PAD_X:
                        continue
                    at = (slice(x_from, x_to), ys, slice(None))
                    shape = (x_to - x_from, ny, LANES)
                    east[at] = wide[:, 256 * g : 256 * g + 128].reshape(shape)
                    north[at] = wide[:, 256 * g + 128 : 256 * g + 256].reshape(shape)

    pack(0)
    pl.semaphore_wait(barrier, len(neighbours) + len(partners))
    halo = [halo_copy(0, k) for k in range(8)]
    for copy in halo:
        copy.start()

    def weight_copies(j):
        copies = [
            pltpu.make_async_remote_copy(
                src_ref=small_ref,
                dst_ref=small.at[sect],
                send_sem=small_send.at[j],
                recv_sem=small_recv.at[j],
                device_id=partners[j],
                device_id_type=MESH,
            )
        ]
        for layer in range(LAYERS):
            part = pl.ds(3 * layer, 3)
            copies.append(
                pltpu.make_async_remote_copy(
                    src_ref=conv_ref.at[part],
                    dst_ref=conv.at[sect, part],
                    send_sem=weight_send.at[j, layer],
                    recv_sem=weight_recv.at[j, layer],
                    device_id=partners[j],
                    device_id_type=MESH,
                )
            )
        return copies

    weights = [weight_copies(j) for j in range(3)]
    for i in range(LAYERS + 1):
        for j in range(3):
            weights[j][i].start()

    regimes = regime_ref[...]
    member = jnp.where(regimes == iota((256, LANES), 1), 1.0, 0.0)
    earlier = jnp.where(iota((256, 256), 1) < iota((256, 256), 0), 1.0, 0.0).astype(BF16)
    place = member * dot(earlier, member.astype(BF16))
    counts = jnp.sum(member, axis=0, keepdims=True)
    tiles = jnp.floor((counts + (TILE - 1)) * (1.0 / TILE))
    before = jnp.where(iota((LANES, LANES), 0) < iota((LANES, LANES), 1), 1.0, 0.0).astype(BF16)
    starts = dot(jnp.broadcast_to(tiles, (8, LANES)).astype(BF16), before)[0:1, :]
    start = member * starts
    slot_column = jnp.sum(place + TILE * start, axis=1, keepdims=True)
    ones = jnp.ones((8, LANES), BF16)
    slot_row = (dot_nt(ones, place.astype(BF16)) + TILE * dot_nt(ones, start.astype(BF16)))[0:1, :]
    unpick[...] = jnp.where(
        slot_column == iota((256, PAD_SLOTS), 1).astype(F32), 1.0, 0.0
    ).astype(BF16)
    pick[...] = jnp.where(
        slot_row == iota((PAD_SLOTS, 256), 0).astype(F32), 1.0, 0.0
    ).astype(BF16)
    answers[SLOTS:, :] = jnp.zeros((PAD_SLOTS - SLOTS, LANES), BF16)
    ends = []
    used = 0
    for r in range(REGIMES - 1):
        named = jnp.sum(jnp.where(regimes == r, 1, 0))
        used = used + (named + (TILE - 1)) // TILE
        ends.append(used)

    def network(tile_index, carry):
        regime = sum(jnp.where(tile_index >= end, 1, 0) for end in ends)
        at = pl.ds(pl.multiple_of(tile_index * TILE, TILE), TILE)
        columns = ordered[at, :]
        level_of = iota((TILE, LANES), 1) % LEVELS
        zero = jnp.zeros((TILE, LANES), BF16)
        masked = [jnp.where(level_of == m, columns, zero) for m in range(LEVELS)]
        lift = lift_map[regime]
        square = jnp.zeros((LANES, LANES), BF16)

        def beside(a, b):
            return jnp.concatenate([a, b], axis=1)

        def over(a, b):
            return jnp.concatenate([a, b], axis=0)

        rows = jnp.concatenate([beside(masked[m], masked[m + 1]) for m in range(0, LEVELS, 2)], axis=0)
        lifted = dot(rows, over(beside(lift, square), beside(square, lift)))
        hidden = [
            lifted[(m // 2) * TILE : (m // 2 + 1) * TILE, (m % 2) * LANES : (m % 2 + 1) * LANES]
            for m in range(LEVELS)
        ]
        for layer in range(LAYERS):
            spacing = 2**layer
            below, centre, above = (conv[regime, 3 * layer + t] for t in range(3))
            active = []
            for m in range(LEVELS):
                u = 0.5 * hidden[m]
                active.append((u + u * jnp.tanh(u)).astype(BF16))
            low = [m for m in range(LEVELS) if (m // spacing) % 2 == 0]
            inner = jnp.concatenate([beside(active[m], active[m + spacing]) for m in low], axis=0)
            result = dot_nt(inner, over(beside(centre, above), beside(below, centre)))
            if 2 * spacing < LEVELS:
                outer = jnp.concatenate(
                    [
                        beside(
                            active[m - spacing] if m >= spacing else zero,
                            active[m + 2 * spacing] if m + 2 * spacing < LEVELS else zero,
                        )
                        for m in low
                    ],
                    axis=0,
                )
                result = result + dot_nt(outer, over(beside(below, square), beside(square, above)))
            for p, m in enumerate(low):
                rows_of = slice(p * TILE, (p + 1) * TILE)
                hidden[m] = hidden[m] + result[rows_of, :LANES]
                hidden[m + spacing] = hidden[m + spacing] + result[rows_of, LANES:]
        rounded = [h.astype(BF16) for h in hidden]
        rows = jnp.concatenate([beside(rounded[m], rounded[m + 1]) for m in range(0, LEVELS, 2)], axis=0)
        mapped = out_map[regime]
        result = dot_nt(rows, over(beside(mapped, square), beside(square, mapped)))
        answer = jnp.zeros((TILE, LANES), F32)
        for m in range(LEVELS):
            piece = result[(m // 2) * TILE : (m // 2 + 1) * TILE, (m % 2) * LANES : (m % 2 + 1) * LANES]
            answer = jnp.where(level_of == m, piece, answer)
        answers[at, :] = answer.astype(BF16)
        return carry

    own = (slice(X0, X0 + SIDE), slice(Y0, Y0 + SIDE), slice(None))
    for step in range(STEPS):
        if step:
            pack(step)
            halo = [halo_copy(step, k) for k in range(8)]
            for copy in halo:
                copy.start()
        for copy in halo:
            copy.wait_recv()
        unpack(step)
        xs, ys = slice(X0 - 4, X0 + SIDE + 4), slice(Y0 - 4, Y0 + SIDE + 4)
        first[xs, ys, :] = field[xs, ys, :] + (1.0 / 6.0) * local_tendency(
            field, east, north, flux, xs, ys
        )
        xs, ys = slice(X0 - 2, X0 + SIDE + 2), slice(Y0 - 2, Y0 + SIDE + 2)
        second[xs, ys, :] = (
            0.75 * field[xs, ys, :]
            + 0.25 * first[xs, ys, :]
            + (0.25 / 6.0) * local_tendency(first, east, north, flux, xs, ys)
        )
        xs, ys = own[0], own[1]
        dyn = (
            (1.0 / 3.0) * field[own]
            + (2.0 / 3.0) * second[own]
            + (1.0 / 9.0) * local_tendency(second, east, north, flux, xs, ys)
        ).reshape(SIDE * SIDE, LANES)
        ordered[...] = dot(pick[0:SLOTS, :], dyn.astype(BF16)).astype(BF16)
        if step == 0:
            for copy in own_copies:
                copy.wait()
            for j in range(3):
                for copy in weights[j]:
                    copy.wait_recv()
            row, column = iota((LANES, 16), 0), iota((LANES, 16), 1)
            to_lift = jnp.where(row // LEVELS == column, 1.0, 0.0).astype(BF16)
            to_out = jnp.where(row // LEVELS + VARS == column, 1.0, 0.0).astype(BF16)
            for r in range(REGIMES):
                lift_map[r] = dot(to_lift, small[r]).astype(BF16)
                out_map[r] = dot(to_out, small[r]).astype(BF16)
        lax.fori_loop(0, TILES, network, 0)
        final = dyn + dot(unpick[...], answers[...])
        if step == STEPS - 1:
            out_ref[...] = final
        else:
            field[own] = final.reshape(SIDE, SIDE, LANES)
        for copy in halo:
            copy.wait_send()
    for j in range(3):
        for copy in weights[j]:
            copy.wait_send()


def per_device(state, winds, regime_table, emu_lift, emu_conv, emu_output):
    cells = SIDE * SIDE
    columns = state.transpose(2, 3, 0, 1).reshape(cells, LANES)
    packed = (
        winds.astype(BF16)
        .reshape(2, LEVELS, 4, 4, SIDE)
        .transpose(3, 4, 0, 2, 1)
        .reshape(4 * SIDE, LANES)
    )
    regimes = regime_table.reshape(cells, 1)
    small = jnp.concatenate([emu_lift[0].T, emu_output[0]], axis=0)
    taps = emu_conv.reshape(3 * LAYERS, LANES, LANES)
    padded = pltpu.VMEM((PAD_X, PAD_Y, LANES), F32)
    dma = pltpu.SemaphoreType.DMA
    result = pl.pallas_call(
        kernel,
        out_shape=jax.ShapeDtypeStruct((cells, LANES), F32),
        in_specs=[pl.BlockSpec(memory_space=pltpu.VMEM)] * 3
        + [pl.BlockSpec(memory_space=pltpu.VMEM), pl.BlockSpec(memory_space=pl.ANY)],
        out_specs=pl.BlockSpec(memory_space=pltpu.VMEM),
        scratch_shapes=[
            padded, padded, padded, padded, padded,
            pltpu.VMEM((24, PAD_Y, LANES), F32),
            pltpu.VMEM((STEPS, 2, 128, LANES), BF16),
            pltpu.VMEM((STEPS, 2, 128, LANES), BF16),
            pltpu.VMEM((STEPS, 2, 160, LANES), BF16),
            pltpu.VMEM((STEPS, 2, 160, LANES), BF16),
            pltpu.VMEM((STEPS, 4, 48, LANES), BF16),
            pltpu.VMEM((STEPS, 4, 48, LANES), BF16),
            pltpu.VMEM((REGIMES, 3 * LAYERS, LANES, LANES), BF16),
            pltpu.VMEM((REGIMES, 16, LANES), BF16),
            pltpu.VMEM((REGIMES, LANES, LANES), BF16),
            pltpu.VMEM((REGIMES, LANES, LANES), BF16),
            pltpu.VMEM((LANES, 8 * LANES), BF16),
            pltpu.VMEM((PAD_SLOTS, cells), BF16),
            pltpu.VMEM((cells, PAD_SLOTS), BF16),
            pltpu.VMEM((SLOTS, LANES), BF16),
            pltpu.VMEM((PAD_SLOTS, LANES), BF16),
            dma((STEPS, 8)), dma((STEPS, 8)),
            dma((3, LAYERS)), dma((3, LAYERS)),
            dma((3,)), dma((3,)),
            dma((2,)),
        ],
        compiler_params=pltpu.CompilerParams(
            collective_id=0, has_side_effects=True, vmem_limit_bytes=32 * 2**20
        ),
    )(columns, packed, regimes, small, taps)
    return result.reshape(SIDE, SIDE, VARS, LEVELS).transpose(2, 3, 0, 1)


def solution(mesh):
    in_specs = (
        P(None, None, "tile", ("sect", "emu")),
        P(None, None, "tile", ("sect", "emu")),
        P("tile", ("sect", "emu"), None, None),
        P("sect", None, None),
        P("sect", None, None, None, None),
        P("sect", None, None),
    )
    out_specs = P(None, None, "tile", ("sect", "emu"))
    return jax.shard_map(
        per_device, mesh=mesh, in_specs=in_specs, out_specs=out_specs, check_vma=False
    )
```

profile of v0, /device:TPU:1, one launch (start us, length us, event | category | flops | bytes accessed | tf_op | source)
XLA Modules:
  0.0 65.6 jit_solution(6780192731735177972)
XLA Ops:
  0.0 0.0 copy-start.3
  0.0 0.0 copy-start.2
  0.0 0.7 %copy-done.3 = bf16[1,128,8]{1,2,0:T(8,128)(2,1)S(1)} copy-done((bf16[1,128,8]{1,2,0:T(8,128)(2,1)S(1)}, bf16[1,128,8]{1,2,0:T(8,128)(2,1)}, u32[]{:S(2)}) %copy-start.3) | copy-done | bytes 2072
  0.7 0.0 copy-done.2
  0.7 1.6 %reshape.24 = f32[256,128]{0,1:T(8,128)S(1)} reshape(f32[16,16,8,16]{1,0,3,2:T(8,128)} %bitcast.15) | data formatting | bytes 262144 | tf_op jit(solution)/shard_map/reshape | solution.py:389
  2.3 0.0 copy-start.1
  2.3 0.1 copy.14.state_ref
  2.4 0.8 %copy-done.1 = f32[2,16,16,16]{3,2,1,0:T(8,128)S(1)} copy-done((f32[2,16,16,16]{3,2,1,0:T(8,128)S(1)}, f32[2,16,16,16]{3,2,1,0:T(8,128)}, u32[]{:S(2)}) %copy-start.1) | copy-done | bytes 32792
  3.3 0.0 copy-start
  3.3 0.2 copy.11
  3.5 0.0 copy-start.4
  3.5 0.1 reshape.20.wind_ref
  3.6 0.5 copy-done.4
  4.2 0.1 copy.12.regime_ref
  4.3 0.0 copy-done
  4.3 59.5 %shard_map.64 = f32[256,128]{1,0:T(8,128)S(1)} custom-call(f32[256,128]{1,0:T(8,128)S(1)} %copy.14.state_ref, bf16[64,128]{1,0:T(8,128)(2,1)S(1)} %reshape.20.wind_ref, s32[256,1]{1,0:T(8,128)S(1)} %copy.12.regime_ref, bf16[16,128]{1,0:T(8,128)(2,1)S(1)} %pad_maximum_fusion.small_ref, bf16[12,128,128]{2,1,0:T(8,128)(2,1)S(1)} %bitcast.14), custom_call_target="tpu_custom_call" | custom-call | tf_op jit(solution)/shard_map/pallas_call | solution.py:401
  63.8 0.3 reshape.23
  64.1 1.5 %copy.13 = f32[16,16,8,16]{1,0,3,2:T(8,128)} copy(f32[16,16,8,16]{3,2,1,0:T(8,128)S(1)} %reshape.23) | data formatting | bytes 262144 | tf_op jit(solution)/shard_map/reshape | solution.py:434
  (2 shorter events, 0.0 us)
Async XLA Ops:
  0.0 0.7 %copy-start.3 = (bf16[1,128,8]{1,2,0:T(8,128)(2,1)S(1)}, bf16[1,128,8]{1,2,0:T(8,128)(2,1)}, u32[]{:S(2)}) copy-start(bf16[1,128,8]{1,2,0:T(8,128)(2,1)} %param.9) | copy-start | bytes 6148
  0.0 0.7 %copy-start.2 = (bf16[1,8,128]{2,1,0:T(8,128)(2,1)S(1)}, bf16[1,8,128]{2,1,0:T(8,128)(2,1)}, u32[]{:S(2)}) copy-start(bf16[1,8,128]{2,1,0:T(8,128)(2,1)} %param.11) | copy-start | bytes 6148
  2.3 0.9 %copy-start.1 = (f32[2,16,16,16]{3,2,1,0:T(8,128)S(1)}, f32[2,16,16,16]{3,2,1,0:T(8,128)}, u32[]{:S(2)}) copy-start(f32[2,16,16,16]{3,2,1,0:T(8,128)} %param.7) | copy-start | bytes 98308
  3.3 1.1 %copy-start = (bf16[1,4,3,128,128]{4,3,2,1,0:T(8,128)(2,1)S(1)}, bf16[1,4,3,128,128]{4,3,2,1,0:T(8,128)(2,1)}, u32[]{:S(2)}) copy-start(bf16[1,4,3,128,128]{4,3,2,1,0:T(8,128)(2,1)} %param.10) | copy-start | bytes 1179652
  3.5 0.7 %copy-start.4 = (s32[1,1,256,1]{2,3,1,0:T(1,128)S(1)}, s32[1,1,256,1]{2,3,1,0:T(1,128)}, u32[]{:S(2)}) copy-start(s32[1,1,256,1]{2,3,1,0:T(1,128)} %param.8) | copy-start | bytes 3076
where the time goes:
time: 65.8 us; the launch traced here: 65.6 us
  Pallas kernels  59.5 us (90%)
  local copies, waits for them, and re-layouts  6.05 us (9%)
    pallas_call x1, Pallas kernels, per_device(): pl.pallas_call(kernel, out_shape=jax.ShapeDtypeStruct((cells, LANES), F32...  59.5 us
    unnamed x10, local copies, waits for them, and re-layouts  2.09 us
    reshape x2, local copies, waits for them, and re-layouts, per_device(): return result.reshape(SIDE, SIDE, VARS, LEVELS).transpose(2, 3, 0, 1)  1.8 us
    reshape x2, local copies, waits for them, and re-layouts, per_device(): columns = state.transpose(2, 3, 0, 1).reshape(cells, LANES)  1.7 us

commit v1 on v0

--- a/solution.py
+++ b/solution.py
@@ -16,9 +16,9 @@
 REGIMES = 4
 LAYERS = 4
 TILE = 32
-TILES = 11
+TILES = 12
+GROUP = 4
 SLOTS = TILES * TILE
-PAD_SLOTS = 384
 X0, Y0 = 6, 8
 PAD_X, PAD_Y = 28, 32
 DIRECTIONS = ((1, 0), (-1, 0), (0, 1), (0, -1), (1, 1), (1, -1), (-1, 1), (-1, -1))
@@ -109,7 +109,7 @@
     field, first, second, east, north, flux,
     send_x, recv_x, send_y, recv_y, send_c, recv_c,
     conv, small, lift_map, out_map, spread, pick, unpick, ordered, answers,
-    halo_send, halo_recv, weight_send, weight_recv, small_send, small_recv, own_sem,
+    halo_send, halo_recv, weight_send, weight_recv, small_send, small_recv,
 ):
     count_tile, count_sect, count_emu = (lax.axis_size(n) for n in ("tile", "sect", "emu"))
     tile, sect, emu = (lax.axis_index(n) for n in ("tile", "sect", "emu"))
@@ -134,12 +134,8 @@
     for device in (*neighbours, *partners):
         pl.semaphore_signal(barrier, inc=1, device_id=device, device_id_type=MESH)
 
-    own_copies = [
-        pltpu.make_async_copy(conv_ref, conv.at[sect], own_sem.at[0]),
-        pltpu.make_async_copy(small_ref, small.at[sect], own_sem.at[1]),
-    ]
-    for copy in own_copies:
-        copy.start()
+    conv[sect] = 0.5 * conv_ref[...]
+    small[sect] = small_ref[...]
 
     row, column = iota((LANES, 8 * LANES), 0), iota((LANES, 8 * LANES), 1)
     group, part = column // (2 * LANES), (column // LANES) % 2
@@ -220,7 +216,7 @@
     def weight_copies(j):
         copies = [
             pltpu.make_async_remote_copy(
-                src_ref=small_ref,
+                src_ref=small.at[sect],
                 dst_ref=small.at[sect],
                 send_sem=small_send.at[j],
                 recv_sem=small_recv.at[j],
@@ -232,7 +228,7 @@
             part = pl.ds(3 * layer, 3)
             copies.append(
                 pltpu.make_async_remote_copy(
-                    src_ref=conv_ref.at[part],
+                    src_ref=conv.at[sect, part],
                     dst_ref=conv.at[sect, part],
                     send_sem=weight_send.at[j, layer],
                     recv_sem=weight_recv.at[j, layer],
@@ -260,12 +256,11 @@
     ones = jnp.ones((8, LANES), BF16)
     slot_row = (dot_nt(ones, place.astype(BF16)) + TILE * dot_nt(ones, start.astype(BF16)))[0:1, :]
     unpick[...] = jnp.where(
-        slot_column == iota((256, PAD_SLOTS), 1).astype(F32), 1.0, 0.0
+        slot_column == iota((256, SLOTS), 1).astype(F32), 1.0, 0.0
     ).astype(BF16)
     pick[...] = jnp.where(
-        slot_row == iota((PAD_SLOTS, 256), 0).astype(F32), 1.0, 0.0
+        slot_row == iota((SLOTS, 256), 0).astype(F32), 1.0, 0.0
     ).astype(BF16)
-    answers[SLOTS:, :] = jnp.zeros((PAD_SLOTS - SLOTS, LANES), BF16)
     ends = []
     used = 0
     for r in range(REGIMES - 1):
@@ -273,63 +268,82 @@
         used = used + (named + (TILE - 1)) // TILE
         ends.append(used)
 
-    def network(tile_index, carry):
-        regime = sum(jnp.where(tile_index >= end, 1, 0) for end in ends)
-        at = pl.ds(pl.multiple_of(tile_index * TILE, TILE), TILE)
+    level_of = iota((TILE, LANES), 1) % LEVELS
+    zero = jnp.zeros((TILE, LANES), BF16)
+    square = jnp.zeros((LANES, LANES), BF16)
+
+    def beside(a, b):
+        return jnp.concatenate([a, b], axis=1)
+
+    def over(a, b):
+        return jnp.concatenate([a, b], axis=0)
+
+    def in_pairs(levels):
+        return jnp.concatenate([beside(levels[m], levels[m + 1]) for m in range(0, LEVELS, 2)], axis=0)
+
+    def out_of_pairs(rows):
+        return [
+            rows[(m // 2) * TILE : (m // 2 + 1) * TILE, (m % 2) * LANES : (m % 2 + 1) * LANES]
+            for m in range(LEVELS)
+        ]
+
+    def lifted(regime, at):
         columns = ordered[at, :]
-        level_of = iota((TILE, LANES), 1) % LEVELS
-        zero = jnp.zeros((TILE, LANES), BF16)
         masked = [jnp.where(level_of == m, columns, zero) for m in range(LEVELS)]
         lift = lift_map[regime]
-        square = jnp.zeros((LANES, LANES), BF16)
-
-        def beside(a, b):
-            return jnp.concatenate([a, b], axis=1)
-
-        def over(a, b):
-            return jnp.concatenate([a, b], axis=0)
-
-        rows = jnp.concatenate([beside(masked[m], masked[m + 1]) for m in range(0, LEVELS, 2)], axis=0)
-        lifted = dot(rows, over(beside(lift, square), beside(square, lift)))
-        hidden = [
-            lifted[(m // 2) * TILE : (m // 2 + 1) * TILE, (m % 2) * LANES : (m % 2 + 1) * LANES]
-            for m in range(LEVELS)
-        ]
-        for layer in range(LAYERS):
-            spacing = 2**layer
-            below, centre, above = (conv[regime, 3 * layer + t] for t in range(3))
-            active = []
-            for m in range(LEVELS):
-                u = 0.5 * hidden[m]
-                active.append((u + u * jnp.tanh(u)).astype(BF16))
-            low = [m for m in range(LEVELS) if (m // spacing) % 2 == 0]
-            inner = jnp.concatenate([beside(active[m], active[m + spacing]) for m in low], axis=0)
-            result = dot_nt(inner, over(beside(centre, above), beside(below, centre)))
-            if 2 * spacing < LEVELS:
-                outer = jnp.concatenate(
-                    [
-                        beside(
-                            active[m - spacing] if m >= spacing else zero,
-                            active[m + 2 * spacing] if m + 2 * spacing < LEVELS else zero,
-                        )
-                        for m in low
-                    ],
+        return out_of_pairs(dot(in_pairs(masked), over(beside(lift, square), beside(square, lift))))
+
+    def convolved(regime, layer, active):
+        spacing = 2**layer
+        below, centre, above = (conv[regime, 3 * layer + t] for t in range(3))
+        low = [m for m in range(LEVELS) if (m // spacing) % 2 == 0]
+        pieces = [jnp.concatenate([active[m] for m in low], axis=0)]
+        pieces.append(jnp.concatenate([active[m + spacing] for m in low], axis=0))
+        taps = over(beside(centre, above), beside(below, centre))
+        if 2 * spacing < LEVELS:
+            pieces.append(
+                jnp.concatenate([active[m - spacing] if m >= spacing else zero for m in low], axis=0)
+            )
+            pieces.append(
+                jnp.concatenate(
+                    [active[m + 2 * spacing] if m + 2 * spacing < LEVELS else zero for m in low],
                     axis=0,
                 )
-                result = result + dot_nt(outer, over(beside(below, square), beside(square, above)))
-            for p, m in enumerate(low):
-                rows_of = slice(p * TILE, (p + 1) * TILE)
-                hidden[m] = hidden[m] + result[rows_of, :LANES]
-                hidden[m + spacing] = hidden[m + spacing] + result[rows_of, LANES:]
-        rounded = [h.astype(BF16) for h in hidden]
-        rows = jnp.concatenate([beside(rounded[m], rounded[m + 1]) for m in range(0, LEVELS, 2)], axis=0)
-        mapped = out_map[regime]
-        result = dot_nt(rows, over(beside(mapped, square), beside(square, mapped)))
-        answer = jnp.zeros((TILE, LANES), F32)
-        for m in range(LEVELS):
-            piece = result[(m // 2) * TILE : (m // 2 + 1) * TILE, (m % 2) * LANES : (m % 2 + 1) * LANES]
-            answer = jnp.where(level_of == m, piece, answer)
-        answers[at, :] = answer.astype(BF16)
+            )
+            taps = beside(taps, over(beside(below, square), beside(square, above)))
+        result = dot_nt(jnp.concatenate(pieces, axis=1), taps)
+        added = [None] * LEVELS
+        for p, m in enumerate(low):
+            rows = slice(p * TILE, (p + 1) * TILE)
+            added[m] = result[rows, :LANES]
+            added[m + spacing] = result[rows, LANES:]
+        return added
+
+    def network(group_index, carry):
+        places, states = [], []
+        for j in range(GROUP):
+            tile_index = group_index * GROUP + j
+            regime = sum(jnp.where(tile_index >= end, 1, 0) for end in ends)
+            at = pl.ds(pl.multiple_of(tile_index * TILE, TILE), TILE)
+            places.append((regime, at))
+            states.append(lifted(regime, at))
+        for layer in range(LAYERS):
+            for j in range(GROUP):
+                active = []
+                for half in states[j]:
+                    u = half.astype(BF16)
+                    active.append(u + u * jnp.tanh(u))
+                added = convolved(places[j][0], layer, active)
+                states[j] = [h + a for h, a in zip(states[j], added)]
+        for j in range(GROUP):
+            regime, at = places[j]
+            mapped = out_map[regime]
+            rows = in_pairs([h.astype(BF16) for h in states[j]])
+            pieces = out_of_pairs(dot_nt(rows, over(beside(mapped, square), beside(square, mapped))))
+            answer = jnp.zeros((TILE, LANES), F32)
+            for m in range(LEVELS):
+                answer = jnp.where(level_of == m, pieces[m], answer)
+            answers[at, :] = answer.astype(BF16)
         return carry
 
     own = (slice(X0, X0 + SIDE), slice(Y0, Y0 + SIDE), slice(None))
@@ -358,20 +372,18 @@
             + (2.0 / 3.0) * second[own]
             + (1.0 / 9.0) * local_tendency(second, east, north, flux, xs, ys)
         ).reshape(SIDE * SIDE, LANES)
-        ordered[...] = dot(pick[0:SLOTS, :], dyn.astype(BF16)).astype(BF16)
+        ordered[...] = dot(pick[...], dyn.astype(BF16)).astype(BF16)
         if step == 0:
-            for copy in own_copies:
-                copy.wait()
             for j in range(3):
                 for copy in weights[j]:
                     copy.wait_recv()
             row, column = iota((LANES, 16), 0), iota((LANES, 16), 1)
-            to_lift = jnp.where(row // LEVELS == column, 1.0, 0.0).astype(BF16)
-            to_out = jnp.where(row // LEVELS + VARS == column, 1.0, 0.0).astype(BF16)
+            to_lift = jnp.where(row // LEVELS == column, 0.5, 0.0).astype(BF16)
+            to_out = jnp.where(row // LEVELS + VARS == column, 2.0, 0.0).astype(BF16)
             for r in range(REGIMES):
                 lift_map[r] = dot(to_lift, small[r]).astype(BF16)
                 out_map[r] = dot(to_out, small[r]).astype(BF16)
-        lax.fori_loop(0, TILES, network, 0)
+        lax.fori_loop(0, TILES // GROUP, network, 0)
         final = dyn + dot(unpick[...], answers[...])
         if step == STEPS - 1:
             out_ref[...] = final
@@ -401,8 +413,7 @@
     result = pl.pallas_call(
         kernel,
         out_shape=jax.ShapeDtypeStruct((cells, LANES), F32),
-        in_specs=[pl.BlockSpec(memory_space=pltpu.VMEM)] * 3
-        + [pl.BlockSpec(memory_space=pltpu.VMEM), pl.BlockSpec(memory_space=pl.ANY)],
+        in_specs=[pl.BlockSpec(memory_space=pltpu.VMEM)] * 5,
         out_specs=pl.BlockSpec(memory_space=pltpu.VMEM),
         scratch_shapes=[
             padded, padded, padded, padded, padded,
@@ -418,14 +429,13 @@
             pltpu.VMEM((REGIMES, LANES, LANES), BF16),
             pltpu.VMEM((REGIMES, LANES, LANES), BF16),
             pltpu.VMEM((LANES, 8 * LANES), BF16),
-            pltpu.VMEM((PAD_SLOTS, cells), BF16),
-            pltpu.VMEM((cells, PAD_SLOTS), BF16),
+            pltpu.VMEM((SLOTS, cells), BF16),
+            pltpu.VMEM((cells, SLOTS), BF16),
             pltpu.VMEM((SLOTS, LANES), BF16),
-            pltpu.VMEM((PAD_SLOTS, LANES), BF16),
+            pltpu.VMEM((SLOTS, LANES), BF16),
             dma((STEPS, 8)), dma((STEPS, 8)),
             dma((3, LAYERS)), dma((3, LAYERS)),
             dma((3,)), dma((3,)),
-            dma((2,)),
         ],
         compiler_params=pltpu.CompilerParams(
             collective_id=0, has_side_effects=True, vmem_limit_bytes=32 * 2**20

time: 65.8 us -> 49 us (0.74)
  Pallas kernels: 59.5 us -> 42.7 us
    pallas_call x1, Pallas kernels: 59.5 us -> 42.7 us  [per_device(): pl.pallas_call(kernel, out_shape=jax.ShapeDtypeStruct((cells, LANES), F32...]
where the time goes in v1:
time: 49 us; the launch traced here: 48.8 us
  Pallas kernels  42.7 us (87%)
  local copies, waits for them, and re-layouts  6.05 us (12%)
    pallas_call x1, Pallas kernels, per_device(): pl.pallas_call(kernel, out_shape=jax.ShapeDtypeStruct((cells, LANES), F32...  42.7 us
    unnamed x10, local copies, waits for them, and re-layouts  2.09 us
    reshape x2, local copies, waits for them, and re-layouts, per_device(): return result.reshape(SIDE, SIDE, VARS, LEVELS).transpose(2, 3, 0, 1)  1.8 us
    reshape x2, local copies, waits for them, and re-layouts, per_device(): columns = state.transpose(2, 3, 0, 1).reshape(cells, LANES)  1.7 us

profile of v1, /device:TPU:1, one launch (start us, length us, event | category | flops | bytes accessed | tf_op | source)
XLA Modules:
  0.0 48.8 jit_solution(4477205904407940857)
XLA Ops:
  0.0 0.0 copy-start.3
  0.0 0.0 copy-start.2
  0.0 0.7 %copy-done.3 = bf16[1,128,8]{1,2,0:T(8,128)(2,1)S(1)} copy-done((bf16[1,128,8]{1,2,0:T(8,128)(2,1)S(1)}, bf16[1,128,8]{1,2,0:T(8,128)(2,1)}, u32[]{:S(2)}) %copy-start.3) | copy-done | bytes 2072
  0.7 0.0 copy-done.2
  0.7 1.6 %reshape.24 = f32[256,128]{0,1:T(8,128)S(1)} reshape(f32[16,16,8,16]{1,0,3,2:T(8,128)} %bitcast.15) | data formatting | bytes 262144 | tf_op jit(solution)/shard_map/reshape | solution.py:401
  2.3 0.0 copy-start.1
  2.3 0.1 copy.14.state_ref
  2.4 0.8 %copy-done.1 = f32[2,16,16,16]{3,2,1,0:T(8,128)S(1)} copy-done((f32[2,16,16,16]{3,2,1,0:T(8,128)S(1)}, f32[2,16,16,16]{3,2,1,0:T(8,128)}, u32[]{:S(2)}) %copy-start.1) | copy-done | bytes 32792
  3.3 0.0 copy-start
  3.3 0.2 copy.11
  3.5 0.0 copy-start.4
  3.5 0.1 reshape.20.wind_ref
  3.6 0.5 %copy-done.4 = s32[1,1,256,1]{2,3,1,0:T(1,128)S(1)} copy-done((s32[1,1,256,1]{2,3,1,0:T(1,128)S(1)}, s32[1,1,256,1]{2,3,1,0:T(1,128)}, u32[]{:S(2)}) %copy-start.4) | copy-done | bytes 1048
  4.2 0.1 copy.12.regime_ref
  4.3 0.0 copy-done
  4.3 42.7 %shard_map.64 = f32[256,128]{1,0:T(8,128)S(1)} custom-call(f32[256,128]{1,0:T(8,128)S(1)} %copy.14.state_ref, bf16[64,128]{1,0:T(8,128)(2,1)S(1)} %reshape.20.wind_ref, s32[256,1]{1,0:T(8,128)S(1)} %copy.12.regime_ref, bf16[16,128]{1,0:T(8,128)(2,1)S(1)} %pad_maximum_fusion.small_ref, bf16[12,128,128]{2,1,0:T(8,128)(2,1)S(1)} %bitcast.14), custom_call_target="tpu_custom_call" | custom-call | tf_op jit(solution)/shard_map/pallas_call | solution.py:413
  47.0 0.3 reshape.23
  47.3 1.5 %copy.13 = f32[16,16,8,16]{1,0,3,2:T(8,128)} copy(f32[16,16,8,16]{3,2,1,0:T(8,128)S(1)} %reshape.23) | data formatting | bytes 262144 | tf_op jit(solution)/shard_map/reshape | solution.py:444
  (2 shorter events, 0.0 us)
Async XLA Ops:
  0.0 0.7 %copy-start.3 = (bf16[1,128,8]{1,2,0:T(8,128)(2,1)S(1)}, bf16[1,128,8]{1,2,0:T(8,128)(2,1)}, u32[]{:S(2)}) copy-start(bf16[1,128,8]{1,2,0:T(8,128)(2,1)} %param.9) | copy-start | bytes 6148
  0.0 0.7 %copy-start.2 = (bf16[1,8,128]{2,1,0:T(8,128)(2,1)S(1)}, bf16[1,8,128]{2,1,0:T(8,128)(2,1)}, u32[]{:S(2)}) copy-start(bf16[1,8,128]{2,1,0:T(8,128)(2,1)} %param.11) | copy-start | bytes 6148
  2.3 0.9 %copy-start.1 = (f32[2,16,16,16]{3,2,1,0:T(8,128)S(1)}, f32[2,16,16,16]{3,2,1,0:T(8,128)}, u32[]{:S(2)}) copy-start(f32[2,16,16,16]{3,2,1,0:T(8,128)} %param.7) | copy-start | bytes 98308
  3.3 1.1 %copy-start = (bf16[1,4,3,128,128]{4,3,2,1,0:T(8,128)(2,1)S(1)}, bf16[1,4,3,128,128]{4,3,2,1,0:T(8,128)(2,1)}, u32[]{:S(2)}) copy-start(bf16[1,4,3,128,128]{4,3,2,1,0:T(8,128)(2,1)} %param.10) | copy-start | bytes 1179652
  3.5 0.7 %copy-start.4 = (s32[1,1,256,1]{2,3,1,0:T(1,128)S(1)}, s32[1,1,256,1]{2,3,1,0:T(1,128)}, u32[]{:S(2)}) copy-start(s32[1,1,256,1]{2,3,1,0:T(1,128)} %param.8) | copy-start | bytes 3076

commit v2 on v1

v2 whole, which is shorter than its diff:
```python
import functools

import jax
import jax.numpy as jnp
from jax import lax
from jax.experimental import pallas as pl
from jax.experimental.pallas import tpu as pltpu
from jax.sharding import PartitionSpec as P

MESH = pl.DeviceIdType.MESH
STEPS = 2
SIDE = 16
LANES = 128
VARS = 8
LEVELS = 16
REGIMES = 4
LAYERS = 4
TILE = 32
TILES = 11
SLOTS = TILES * TILE
PAD_SLOTS = 384
CORNER = 4
X0, Y0 = 6, 8
PAD_X, PAD_Y = 28, 32
DIRECTIONS = ((1, 1), (1, -1), (-1, 1), (-1, -1), (1, 0), (-1, 0), (0, 1), (0, -1))
BF16 = jnp.bfloat16
F32 = jnp.float32


def dot(a, b):
    return jnp.dot(a, b, preferred_element_type=F32)


def dot_nt(a, b):
    return lax.dot_general(a, b, (((1,), (1,)), ((), ())), preferred_element_type=F32)


def iota(shape, dim):
    return lax.broadcasted_iota(jnp.int32, shape, dim)


def field_rows(dx, dy):
    return 96 if dy == 0 else 128 if dx == 0 else CORNER * CORNER


def wind_rows(dx, dy):
    return 16 if dx and dy else 32


def sent_box(dx, dy):
    deep_x, deep_y = (CORNER, CORNER) if dx and dy else (6, 8)
    xs = slice(X0, X0 + deep_x) if dx < 0 else slice(X0 + SIDE - deep_x, X0 + SIDE)
    ys = slice(Y0, Y0 + deep_y) if dy < 0 else slice(Y0 + SIDE - deep_y, Y0 + SIDE)
    return xs if dx else slice(X0, X0 + SIDE), ys if dy else slice(Y0, Y0 + SIDE)


def moved(box, dx, dy):
    xs, ys = box
    return (
        slice(xs.start - SIDE * dx, xs.stop - SIDE * dx),
        slice(ys.start - SIDE * dy, ys.stop - SIDE * dy),
    )


def wind_groups(dx, dy):
    ys = slice(Y0, Y0 + SIDE) if dy == 0 else slice(Y0 + 8, Y0 + 16) if dy > 0 else slice(Y0, Y0 + 8)
    if dx == 0:
        return [(g, slice(X0 + 4 * g, X0 + 4 * g + 4), ys) for g in range(4)]
    base = X0 + 8 if dx > 0 else X0
    if dy:
        quarters = (2, 3) if dx > 0 else (0, 1)
    else:
        quarters = (1, 2, 3) if dx > 0 else (0, 1, 2)
    return [(g, slice(base + 2 * g, base + 2 * g + 2), ys) for g in quarters]


def local_tendency(src, east, north, flux, xs, ys):
    nx, ny = xs.stop - xs.start, ys.stop - ys.start

    def face_flux(speed, before, center, after, beyond):
        both = 2.0 * (center + after)
        up = jnp.maximum(speed, 0.0)
        down = jnp.minimum(speed, 0.0)
        return up * (both + 3.0 * center - before) + down * (both + 3.0 * after - beyond)

    along_x = src[xs.start - 2 : xs.stop + 2, ys, :]
    flux_x = face_flux(
        east[xs.start - 1 : xs.stop, ys, :],
        along_x[0 : nx + 1],
        along_x[1 : nx + 2],
        along_x[2 : nx + 3],
        along_x[3 : nx + 4],
    )
    total = flux_x[:nx] - flux_x[1:]
    faces = slice(ys.start - 1, ys.stop)
    flux[0:nx, 0 : ny + 1, :] = face_flux(
        north[xs, faces, :],
        src[xs, faces.start - 1 : faces.stop - 1, :],
        src[xs, faces, :],
        src[xs, faces.start + 1 : faces.stop + 1, :],
        src[xs, faces.start + 2 : faces.stop + 2, :],
    )
    return total + (flux[0:nx, 0:ny, :] - flux[0:nx, 1 : ny + 1, :])


def kernel(
    state_ref, wind_ref, regime_ref, lift_ref, output_ref, taps_ref, out_ref,
    state_in, wind_in, regime_in, lift_in, output_in, taps_in,
    field, first, second, east, north, flux, stage,
    send_x, recv_x, send_y, recv_y, send_c, recv_c,
    conv_0, conv_1, conv_2, conv_3, small, lift_map, out_map, spread, pick, unpick, ordered, answers,
    load_sem, halo_send, halo_recv, weight_send, weight_recv, small_send, small_recv,
):
    count_tile, count_sect, count_emu = (lax.axis_size(n) for n in ("tile", "sect", "emu"))
    tile, sect, emu = (lax.axis_index(n) for n in ("tile", "sect", "emu"))
    along_y = sect * count_emu + emu
    total_y = count_sect * count_emu

    def neighbour(dx, dy):
        y = lax.rem(along_y + (dy + total_y), total_y)
        return (lax.rem(tile + (dx + count_tile), count_tile), y // count_emu, lax.rem(y, count_emu))

    half = count_tile // 2
    far_tile = lax.rem(tile + half, count_tile)
    core, chip = lax.rem(sect, 2), sect // 2
    partners = (
        (tile, chip * 2 + (1 - core), emu),
        (tile, (1 - chip) * 2 + core, emu),
        (far_tile, (1 - chip) * 2 + (1 - core), emu),
    )
    neighbours = [neighbour(dx, dy) for dx, dy in DIRECTIONS]

    conv = (conv_0, conv_1, conv_2, conv_3)
    barrier = pltpu.get_barrier_semaphore()
    for device in (*neighbours, *partners):
        pl.semaphore_signal(barrier, inc=1, device_id=device, device_id_type=MESH)

    loads = [
        pltpu.make_async_copy(src, dst, load_sem.at[i])
        for i, (src, dst) in enumerate(
            (
                (wind_ref, wind_in),
                (state_ref, state_in),
                (taps_ref, taps_in),
                (regime_ref, regime_in),
                (lift_ref, lift_in),
                (output_ref, output_in),
            )
        )
    ]
    for copy in loads:
        copy.start()

    row, column = iota((LANES, 8 * LANES), 0), iota((LANES, 8 * LANES), 1)
    group, part = column // (2 * LANES), (column // LANES) % 2
    chosen = (row // LEVELS == part * 4 + group) & (row % LEVELS == column % LEVELS)
    spread[...] = jnp.where(chosen, 1.0, 0.0).astype(BF16)
    loads[0].wait()
    packed = []
    for j in range(4):
        rows = [
            wind_in[pl.ds(c * LEVELS * SIDE + 4 * g + j, LEVELS, stride=SIDE), :]
            for c in range(2)
            for g in range(4)
        ]
        packed.append(jnp.concatenate(rows, axis=0).T)
    wide = dot(jnp.concatenate(packed, axis=0).astype(BF16), spread[...])
    for g in range(4):
        at = (slice(X0 + 4 * g, X0 + 4 * g + 4), slice(Y0, Y0 + SIDE), slice(None))
        east[at] = wide[:, 256 * g : 256 * g + 128].reshape(4, SIDE, LANES)
        north[at] = wide[:, 256 * g + 128 : 256 * g + 256].reshape(4, SIDE, LANES)
    loads[1].wait()
    for x in range(SIDE):
        field[X0 + x, Y0 : Y0 + SIDE, :] = state_in[pl.ds(x, LANES, stride=SIDE), :].T

    def buffers(step, k):
        dx, dy = DIRECTIONS[k]
        if dy == 0:
            return send_x.at[step, k - 4], recv_x.at[step, k - 4]
        if dx == 0:
            return send_y.at[step, k - 6], recv_y.at[step, k - 6]
        return send_c.at[step, k], recv_c.at[step, k]

    def halo_copy(step, k):
        sent, received = buffers(step, k)
        rows = field_rows(*DIRECTIONS[k]) + (wind_rows(*DIRECTIONS[k]) if step == 0 else 0)
        return pltpu.make_async_remote_copy(
            src_ref=sent.at[0:rows],
            dst_ref=received.at[0:rows],
            send_sem=halo_send.at[step, k],
            recv_sem=halo_recv.at[step, k],
            device_id=neighbours[k],
            device_id_type=MESH,
        )

    def pack(step):
        for k, (dx, dy) in enumerate(DIRECTIONS):
            sent, _ = buffers(step, k)
            xs, ys = sent_box(dx, dy)
            rows = field_rows(dx, dy)
            if dx and dy:
                for i in range(CORNER):
                    stage[k, CORNER * i : CORNER * (i + 1), :] = field[xs.start + i, ys, :]
                sent[0:rows, :] = stage[k].astype(BF16)
            else:
                sent[0:rows, :] = field[xs, ys, :].reshape(rows, LANES).astype(BF16)
            if step == 0:
                more = wind_rows(dx, dy)
                quarter = iota((more, LANES), 1) // LEVELS
                packed = jnp.zeros((more, LANES), F32)
                for c, winds in enumerate((east, north)):
                    for g, gx, gy in wind_groups(dx, dy):
                        piece = winds[gx, gy, :].reshape(more, LANES)
                        packed = jnp.where(quarter == c * 4 + g, piece, packed)
                sent[rows : rows + more, :] = packed.astype(BF16)

    def unpack(step):
        for k, (dx, dy) in enumerate(DIRECTIONS):
            _, received = buffers(step, k)
            xs, ys = moved(sent_box(dx, dy), dx, dy)
            rows = field_rows(dx, dy)
            nx, ny = xs.stop - xs.start, ys.stop - ys.start
            if dx and dy:
                stage[k] = received[0:rows, :].astype(F32)
                for i in range(CORNER):
                    field[xs.start + i, ys, :] = stage[k, CORNER * i : CORNER * (i + 1), :]
            else:
                field[xs, ys, :] = received[0:rows, :].astype(F32).reshape(nx, ny, LANES)
            if step == 0:
                more = wind_rows(dx, dy)
                wide = dot(received[rows : rows + more, :], spread[...])
                for g, gx, gy in wind_groups(dx, dy):
                    xs, ys = moved((gx, gy), dx, dy)
                    shape = (xs.stop - xs.start, ys.stop - ys.start, LANES)
                    east[xs, ys, :] = wide[:, 256 * g : 256 * g + 128].reshape(shape)
                    north[xs, ys, :] = wide[:, 256 * g + 128 : 256 * g + 256].reshape(shape)

    pack(0)
    pl.semaphore_wait(barrier, len(neighbours) + len(partners))
    halo = [halo_copy(0, k) for k in range(8)]
    for copy in halo:
        copy.start()

    for copy in loads[2:]:
        copy.wait()
    for layer in range(LAYERS):
        conv[layer][sect] = 0.5 * taps_in[3 * layer : 3 * layer + 3]
    small[sect] = jnp.concatenate([lift_in[...], output_in[...]], axis=0)

    def weight_copies(j):
        copies = [
            pltpu.make_async_remote_copy(
                src_ref=small.at[sect],
                dst_ref=small.at[sect],
                send_sem=small_send.at[j],
                recv_sem=small_recv.at[j],
                device_id=partners[j],
                device_id_type=MESH,
            )
        ]
        for layer in range(LAYERS):
            copies.append(
                pltpu.make_async_remote_copy(
                    src_ref=conv[layer].at[sect],
                    dst_ref=conv[layer].at[sect],
                    send_sem=weight_send.at[j, layer],
                    recv_sem=weight_recv.at[j, layer],
                    device_id=partners[j],
                    device_id_type=MESH,
                )
            )
        return copies

    weights = [weight_copies(j) for j in range(3)]
    for i in range(LAYERS + 1):
        for j in range(3):
            weights[j][i].start()

    regimes = regime_in[...]
    member = jnp.where(regimes == iota((8, 256), 0), 1.0, 0.0)
    earlier = jnp.where(iota((256, 256), 0) < iota((256, 256), 1), 1.0, 0.0).astype(BF16)
    place = member * dot(member.astype(BF16), earlier)
    tiles = jnp.floor((jnp.sum(member, axis=1, keepdims=True) + (TILE - 1)) * (1.0 / TILE))
    before = jnp.where(iota((8, 8), 1) < iota((8, 8), 0), 1.0, 0.0).astype(BF16)
    starts = dot(before, jnp.broadcast_to(tiles, (8, LANES)).astype(BF16))[:, 0:1]
    start = member * starts
    slot_row = jnp.sum(place + TILE * start, axis=0, keepdims=True)
    same = jnp.where(iota((256, 256), 0) == iota((256, 256), 1), 1.0, 0.0).astype(BF16)
    slot_column = jnp.sum(
        dot_nt(same, place.astype(BF16)) + TILE * dot_nt(same, start.astype(BF16)),
        axis=1,
        keepdims=True,
    )
    unpick[...] = jnp.where(
        slot_column == iota((256, PAD_SLOTS), 1).astype(F32), 1.0, 0.0
    ).astype(BF16)
    pick[...] = jnp.where(
        slot_row == iota((SLOTS, 256), 0).astype(F32), 1.0, 0.0
    ).astype(BF16)
    answers[SLOTS:, :] = jnp.zeros((PAD_SLOTS - SLOTS, LANES), BF16)
    tile_regimes = [0] * TILES
    used = 0
    for r in range(REGIMES - 1):
        named = jnp.sum(jnp.where(regimes == r, 1, 0))
        used = used + (named + (TILE - 1)) // TILE
        tile_regimes = [r_of + jnp.where(t >= used, 1, 0) for t, r_of in enumerate(tile_regimes)]

    level_of = iota((TILE, LANES), 1) % LEVELS
    square = jnp.zeros((LANES, LANES), BF16)

    def beside(a, b):
        return jnp.concatenate([a, b], axis=1)

    def over(a, b):
        return jnp.concatenate([a, b], axis=0)

    zero = jnp.zeros((TILE, LANES), BF16)

    def in_pairs(levels):
        return jnp.concatenate([beside(levels[m], levels[m + 1]) for m in range(0, LEVELS, 2)], axis=0)

    def out_of_pairs(rows):
        return [
            rows[m // 2 * TILE : (m // 2 + 1) * TILE, m % 2 * LANES : (m % 2 + 1) * LANES]
            for m in range(LEVELS)
        ]

    def both(tap):
        return over(beside(tap, square), beside(square, tap))

    def lifted(t):
        columns = ordered[t * TILE : (t + 1) * TILE, :]
        masked = [jnp.where(level_of == m, columns, zero) for m in range(LEVELS)]
        return out_of_pairs(dot(in_pairs(masked), both(lift_map[tile_regimes[t]])))

    def layered(t, layer, halves):
        spacing = 2**layer
        below, centre, above = (conv[layer][tile_regimes[t], i] for i in range(3))
        active = []
        for half in halves:
            u = half.astype(BF16)
            active.append(u + u * jnp.tanh(u))
        low = [m for m in range(LEVELS) if m // spacing % 2 == 0]
        pieces = [[active[m] for m in low], [active[m + spacing] for m in low]]
        taps = over(beside(centre, above), beside(below, centre))
        if 2 * spacing < LEVELS:
            pieces.append([active[m - spacing] if m >= spacing else zero for m in low])
            pieces.append(
                [active[m + 2 * spacing] if m + 2 * spacing < LEVELS else zero for m in low]
            )
            taps = beside(taps, over(beside(below, square), beside(square, above)))
        result = dot_nt(
            jnp.concatenate([jnp.concatenate(piece, axis=0) for piece in pieces], axis=1), taps
        )
        halves = list(halves)
        for p, m in enumerate(low):
            rows = slice(p * TILE, (p + 1) * TILE)
            halves[m] = halves[m] + result[rows, :LANES]
            halves[m + spacing] = halves[m + spacing] + result[rows, LANES:]
        return halves

    def answered(t, halves):
        rows = in_pairs([half.astype(BF16) for half in halves])
        pieces = out_of_pairs(dot_nt(rows, both(out_map[tile_regimes[t]])))
        answer = jnp.zeros((TILE, LANES), F32)
        for m in range(LEVELS):
            answer = jnp.where(level_of == m, pieces[m], answer)
        return answer.astype(BF16)

    def network(first_time):
        tiles = [lifted(t) for t in range(TILES)]
        for layer in range(LAYERS):
            if first_time:
                for j in range(3):
                    weights[j][1 + layer].wait_recv()
            tiles = [layered(t, layer, tiles[t]) for t in range(TILES)]
        results = [answered(t, tiles[t]) for t in range(TILES)]
        for t in range(TILES):
            answers[t * TILE : (t + 1) * TILE, :] = results[t]

    own = (slice(X0, X0 + SIDE), slice(Y0, Y0 + SIDE), slice(None))
    for step in range(STEPS):
        if step:
            pack(step)
            halo = [halo_copy(step, k) for k in range(8)]
            for copy in halo:
                copy.start()
        for copy in halo:
            copy.wait_recv()
        unpack(step)
        xs, ys = slice(X0 - 4, X0 + SIDE + 4), slice(Y0 - 4, Y0 + SIDE + 4)
        first[xs, ys, :] = field[xs, ys, :] + (1.0 / 6.0) * local_tendency(
            field, east, north, flux, xs, ys
        )
        xs, ys = slice(X0 - 2, X0 + SIDE + 2), slice(Y0 - 2, Y0 + SIDE + 2)
        second[xs, ys, :] = (
            0.75 * field[xs, ys, :]
            + 0.25 * first[xs, ys, :]
            + (0.25 / 6.0) * local_tendency(first, east, north, flux, xs, ys)
        )
        xs, ys = own[0], own[1]
        dyn = (
            (1.0 / 3.0) * field[own]
            + (2.0 / 3.0) * second[own]
            + (1.0 / 9.0) * local_tendency(second, east, north, flux, xs, ys)
        ).reshape(SIDE * SIDE, LANES)
        ordered[...] = dot(pick[...], dyn.astype(BF16)).astype(BF16)
        if step == 0:
            for j in range(3):
                weights[j][0].wait_recv()
            row, column = iota((LANES, 16), 0), iota((LANES, 16), 1)
            to_lift = jnp.where(row // LEVELS == column, 0.5, 0.0).astype(BF16)
            to_out = jnp.where(row // LEVELS + VARS == column, 2.0, 0.0).astype(BF16)
            for r in range(REGIMES):
                lift_map[r] = dot(to_lift, small[r]).astype(BF16)
                out_map[r] = dot(to_out, small[r]).astype(BF16)
        network(step == 0)
        final = dyn + dot(unpick[...], answers[...])
        if step == STEPS - 1:
            out_ref[...] = final
        else:
            field[own] = final.reshape(SIDE, SIDE, LANES)
        for copy in halo:
            copy.wait_send()
    for j in range(3):
        for copy in weights[j]:
            copy.wait_send()


def per_device(state, winds, regime_table, emu_lift, emu_conv, emu_output):
    cells = SIDE * SIDE
    padded = pltpu.VMEM((PAD_X, PAD_Y, LANES), F32)
    dma = pltpu.SemaphoreType.DMA
    result = pl.pallas_call(
        kernel,
        out_shape=jax.ShapeDtypeStruct((cells, LANES), F32),
        in_specs=[pl.BlockSpec(memory_space=pl.ANY)] * 6,
        out_specs=pl.BlockSpec(memory_space=pltpu.VMEM),
        scratch_shapes=[
            pltpu.VMEM((LANES * SIDE, SIDE), F32),
            pltpu.VMEM((2 * LEVELS * SIDE, SIDE), F32),
            pltpu.VMEM((1, cells), jnp.int32),
            pltpu.VMEM((VARS, LANES), BF16),
            pltpu.VMEM((VARS, LANES), BF16),
            pltpu.VMEM((3 * LAYERS, LANES, LANES), BF16),
            padded, padded, padded, padded, padded,
            pltpu.VMEM((24, PAD_Y, LANES), F32),
            pltpu.VMEM((4, CORNER * CORNER, LANES), F32),
            pltpu.VMEM((STEPS, 2, 128, LANES), BF16),
            pltpu.VMEM((STEPS, 2, 128, LANES), BF16),
            pltpu.VMEM((STEPS, 2, 160, LANES), BF16),
            pltpu.VMEM((STEPS, 2, 160, LANES), BF16),
            pltpu.VMEM((STEPS, 4, 32, LANES), BF16),
            pltpu.VMEM((STEPS, 4, 32, LANES), BF16),
            *[pltpu.VMEM((REGIMES, 3, LANES, LANES), BF16)] * LAYERS,
            pltpu.VMEM((REGIMES, 2 * VARS, LANES), BF16),
            pltpu.VMEM((REGIMES, LANES, LANES), BF16),
            pltpu.VMEM((REGIMES, LANES, LANES), BF16),
            pltpu.VMEM((LANES, 8 * LANES), BF16),
            pltpu.VMEM((SLOTS, cells), BF16),
            pltpu.VMEM((cells, PAD_SLOTS), BF16),
            pltpu.VMEM((SLOTS, LANES), BF16),
            pltpu.VMEM((PAD_SLOTS, LANES), BF16),
            dma((6,)),
            dma((STEPS, 8)), dma((STEPS, 8)),
            dma((3, LAYERS)), dma((3, LAYERS)),
            dma((3,)), dma((3,)),
        ],
        compiler_params=pltpu.CompilerParams(
            collective_id=0, has_side_effects=True, vmem_limit_bytes=60 * 2**20
        ),
    )(
        state.reshape(LANES * SIDE, SIDE),
        winds.reshape(2 * LEVELS * SIDE, SIDE),
        regime_table.reshape(1, cells),
        emu_lift[0].T,
        emu_output[0],
        emu_conv.reshape(3 * LAYERS, LANES, LANES),
    )
    return result.reshape(SIDE, SIDE, VARS, LEVELS).transpose(2, 3, 0, 1)


def solution(mesh):
    in_specs = (
        P(None, None, "tile", ("sect", "emu")),
        P(None, None, "tile", ("sect", "emu")),
        P("tile", ("sect", "emu"), None, None),
        P("sect", None, None),
        P("sect", None, None, None, None),
        P("sect", None, None),
    )
    out_specs = P(None, None, "tile", ("sect", "emu"))
    return jax.shard_map(
        per_device, mesh=mesh, in_specs=in_specs, out_specs=out_specs, check_vma=False
    )
```

time: 49 us -> 42.9 us (0.88)
  local copies, waits for them, and re-layouts: 6.05 us -> 2.71 us
  Pallas kernels: 42.7 us -> 40 us
    pallas_call x1, Pallas kernels: 42.7 us -> 40 us  [per_device(): pl.pallas_call(kernel, out_shape=jax.ShapeDtypeStruct((cells, LANES), F32...]
    reshape x5 -> x0, local copies, waits for them, and re-layouts: 2.16 us -> none  [the longest x2 1.7 us: per_device(): columns = state.transpose(2, 3, 0, 1).reshape(cells, LANES)]
    unnamed x10 -> x0, local copies, waits for them, and re-layouts: 2.09 us -> none
    reshape x2, local copies, waits for them, and re-layouts: 1.8 us -> 2.71 us  [per_device(): return result.reshape(SIDE, SIDE, VARS, LEVELS).transpose(2, 3, 0, 1)]
where the time goes in v2:
time: 42.9 us; the launch traced here: 42.7 us
  Pallas kernels  40 us (93%)
  local copies, waits for them, and re-layouts  2.71 us (6%)
    pallas_call x1, Pallas kernels, per_device(): pl.pallas_call(kernel, out_shape=jax.ShapeDtypeStruct((cells, LANES), F32...  40 us
    reshape x2, local copies, waits for them, and re-layouts, per_device(): return result.reshape(SIDE, SIDE, VARS, LEVELS).transpose(2, 3, 0, 1)  2.71 us

profile of v2, /device:TPU:1, one launch (start us, length us, event | category | flops | bytes accessed | tf_op | source)
XLA Modules:
  0.0 42.7 jit_solution(13009412681286240789)
XLA Ops:
  0.0 40.0 %shard_map.64 = f32[256,128]{1,0:T(8,128)} custom-call(f32[2048,16]{1,0:T(8,128)} %bitcast.9, f32[512,16]{1,0:T(8,128)} %bitcast.11, s32[1,256]{1,0:T(1,128)} %bitcast.14, bf16[8,128]{1,0:T(8,128)(2,1)} %bitcast.12, bf16[8,128]{1,0:T(8,128)(2,1)} %bitcast.13, bf16[12,128,128]{2,1,0:T(8,128)(2,1)} %bitcast.10), custom_call_target="tpu_custom_call" | custom-call | tf_op jit(solution)/shard_map/pallas_call | solution.py:434
  40.0 1.2 %reshape.19 = f32[16,16,8,16]{3,2,1,0:T(8,128)S(1)} reshape(f32[256,128]{1,0:T(8,128)} %shard_map.64) | data formatting | bytes 262144 | tf_op jit(solution)/shard_map/reshape | solution.py:480
  41.3 1.5 %copy.7 = f32[16,16,8,16]{1,0,3,2:T(8,128)} copy(f32[16,16,8,16]{3,2,1,0:T(8,128)S(1)} %reshape.19) | data formatting | bytes 262144 | tf_op jit(solution)/shard_map/reshape | solution.py:480

commit v3 on v2

--- a/solution.py
+++ b/solution.py
@@ -16,12 +16,16 @@
 REGIMES = 4
 LAYERS = 4
 TILE = 32
-TILES = 11
+LATE = 6
+SAFE = SIDE - LATE
+SAFE_TILES, LATE_TILES = 8, 6
+TILES = SAFE_TILES + LATE_TILES
+SAFE_SLOTS = SAFE_TILES * TILE
 SLOTS = TILES * TILE
-PAD_SLOTS = 384
+PAD_SLOTS = 512
 CORNER = 4
-X0, Y0 = 6, 8
-PAD_X, PAD_Y = 28, 32
+X0, Y0 = 8, 8
+PAD_X, PAD_Y = 32, 32
 DIRECTIONS = ((1, 1), (1, -1), (-1, 1), (-1, -1), (1, 0), (-1, 0), (0, 1), (0, -1))
 BF16 = jnp.bfloat16
 F32 = jnp.float32
@@ -54,28 +58,16 @@
     return xs if dx else slice(X0, X0 + SIDE), ys if dy else slice(Y0, Y0 + SIDE)
 
 
-def moved(box, dx, dy):
-    xs, ys = box
-    return (
-        slice(xs.start - SIDE * dx, xs.stop - SIDE * dx),
-        slice(ys.start - SIDE * dy, ys.stop - SIDE * dy),
-    )
-
-
 def wind_groups(dx, dy):
     ys = slice(Y0, Y0 + SIDE) if dy == 0 else slice(Y0 + 8, Y0 + 16) if dy > 0 else slice(Y0, Y0 + 8)
     if dx == 0:
-        return [(g, slice(X0 + 4 * g, X0 + 4 * g + 4), ys) for g in range(4)]
+        return [(slice(X0 + 4 * g, X0 + 4 * g + 4), ys) for g in range(4)]
     base = X0 + 8 if dx > 0 else X0
-    if dy:
-        quarters = (2, 3) if dx > 0 else (0, 1)
-    else:
-        quarters = (1, 2, 3) if dx > 0 else (0, 1, 2)
-    return [(g, slice(base + 2 * g, base + 2 * g + 2), ys) for g in quarters]
-
-
-def local_tendency(src, east, north, flux, xs, ys):
-    nx, ny = xs.stop - xs.start, ys.stop - ys.start
+    return [(slice(base + 2 * g, base + 2 * g + 2), ys) for g in range(4)]
+
+
+def local_tendency(src, east, north, flux, x_from, nx, ys):
+    ny = ys.stop - ys.start
 
     def face_flux(speed, before, center, after, beyond):
         both = 2.0 * (center + after)
@@ -83,22 +75,23 @@
         down = jnp.minimum(speed, 0.0)
         return up * (both + 3.0 * center - before) + down * (both + 3.0 * after - beyond)
 
-    along_x = src[xs.start - 2 : xs.stop + 2, ys, :]
+    along_x = src[pl.ds(x_from - 2, nx + 4), ys, :]
     flux_x = face_flux(
-        east[xs.start - 1 : xs.stop, ys, :],
+        east[pl.ds(x_from - 1, nx + 1), ys, :],
         along_x[0 : nx + 1],
         along_x[1 : nx + 2],
         along_x[2 : nx + 3],
         along_x[3 : nx + 4],
     )
     total = flux_x[:nx] - flux_x[1:]
-    faces = slice(ys.start - 1, ys.stop)
+    xs = pl.ds(x_from, nx)
+    start, stop = ys.start - 1, ys.stop
     flux[0:nx, 0 : ny + 1, :] = face_flux(
-        north[xs, faces, :],
-        src[xs, faces.start - 1 : faces.stop - 1, :],
-        src[xs, faces, :],
-        src[xs, faces.start + 1 : faces.stop + 1, :],
-        src[xs, faces.start + 2 : faces.stop + 2, :],
+        north[xs, start:stop, :],
+        src[xs, start - 1 : stop - 1, :],
+        src[xs, start:stop, :],
+        src[xs, start + 1 : stop + 1, :],
+        src[xs, start + 2 : stop + 2, :],
     )
     return total + (flux[0:nx, 0:ny, :] - flux[0:nx, 1 : ny + 1, :])
 
@@ -108,7 +101,7 @@
     state_in, wind_in, regime_in, lift_in, output_in, taps_in,
     field, first, second, east, north, flux, stage,
     send_x, recv_x, send_y, recv_y, send_c, recv_c,
-    conv_0, conv_1, conv_2, conv_3, small, lift_map, out_map, spread, pick, unpick, ordered, answers,
+    conv_0, conv_1, conv_2, conv_3, small, lift_map, out_map, spread, pick, unpick, ordered, answers, dyn,
     load_sem, halo_send, halo_recv, weight_send, weight_recv, small_send, small_recv,
 ):
     count_tile, count_sect, count_emu = (lax.axis_size(n) for n in ("tile", "sect", "emu"))
@@ -121,6 +114,8 @@
         return (lax.rem(tile + (dx + count_tile), count_tile), y // count_emu, lax.rem(y, count_emu))
 
     half = count_tile // 2
+    upper = lax.rem(tile, half) // (half // 2)
+    safe_from, late_from = LATE * (1 - upper), SAFE * upper
     far_tile = lax.rem(tile + half, count_tile)
     core, chip = lax.rem(sect, 2), sect // 2
     partners = (
@@ -209,31 +204,59 @@
                 quarter = iota((more, LANES), 1) // LEVELS
                 packed = jnp.zeros((more, LANES), F32)
                 for c, winds in enumerate((east, north)):
-                    for g, gx, gy in wind_groups(dx, dy):
+                    for g, (gx, gy) in enumerate(wind_groups(dx, dy)):
                         piece = winds[gx, gy, :].reshape(more, LANES)
                         packed = jnp.where(quarter == c * 4 + g, piece, packed)
                 sent[rows : rows + more, :] = packed.astype(BF16)
 
-    def unpack(step):
-        for k, (dx, dy) in enumerate(DIRECTIONS):
-            _, received = buffers(step, k)
-            xs, ys = moved(sent_box(dx, dy), dx, dy)
-            rows = field_rows(dx, dy)
-            nx, ny = xs.stop - xs.start, ys.stop - ys.start
-            if dx and dy:
-                stage[k] = received[0:rows, :].astype(F32)
-                for i in range(CORNER):
-                    field[xs.start + i, ys, :] = stage[k, CORNER * i : CORNER * (i + 1), :]
-            else:
-                field[xs, ys, :] = received[0:rows, :].astype(F32).reshape(nx, ny, LANES)
+    def arrive(step, k, ref, rows):
+        pltpu.make_async_remote_copy(
+            src_ref=ref.at[0:rows],
+            dst_ref=ref.at[0:rows],
+            send_sem=halo_send.at[step, k],
+            recv_sem=halo_recv.at[step, k],
+            device_id=neighbours[0],
+            device_id_type=MESH,
+        ).wait_recv()
+
+    def unpack_winds(packed, x_from, ys):
+        wide = dot(packed, spread[...])
+        ny = ys.stop - ys.start
+        deep = packed.shape[0] // ny
+        for g in range(4):
+            xs = pl.ds(x_from + deep * g, deep)
+            east[xs, ys, :] = wide[:, 256 * g : 256 * g + 128].reshape(deep, ny, LANES)
+            north[xs, ys, :] = wide[:, 256 * g + 128 : 256 * g + 256].reshape(deep, ny, LANES)
+
+    def receive_y(step):
+        for k, ys in ((6, slice(Y0 - 8, Y0)), (7, slice(Y0 + SIDE, Y0 + SIDE + 8))):
+            rows, more = 128, 32 if step == 0 else 0
+            ref = recv_y.at[step, k - 6]
+            arrive(step, k, ref, rows + more)
+            field[X0 : X0 + SIDE, ys, :] = ref[0:rows, :].astype(F32).reshape(SIDE, 8, LANES)
             if step == 0:
-                more = wind_rows(dx, dy)
-                wide = dot(received[rows : rows + more, :], spread[...])
-                for g, gx, gy in wind_groups(dx, dy):
-                    xs, ys = moved((gx, gy), dx, dy)
-                    shape = (xs.stop - xs.start, ys.stop - ys.start, LANES)
-                    east[xs, ys, :] = wide[:, 256 * g : 256 * g + 128].reshape(shape)
-                    north[xs, ys, :] = wide[:, 256 * g + 128 : 256 * g + 256].reshape(shape)
+                unpack_winds(ref[rows : rows + more, :], X0, ys)
+
+    def receive_x(step, side):
+        rows, more = 96, 32 if step == 0 else 0
+        ref = recv_x.at[step, side]
+        arrive(step, 4 + side, ref, rows + more)
+        own_y = slice(Y0, Y0 + SIDE)
+        xs = pl.ds(X0 - 6 + (SIDE + 6) * side, 6)
+        field[xs, own_y, :] = ref[0:rows, :].astype(F32).reshape(6, SIDE, LANES)
+        winds_from = X0 - 8 + (SIDE + 8) * side
+        if step == 0:
+            unpack_winds(ref[rows : rows + more, :], winds_from, own_y)
+        x_from = X0 - CORNER + (SIDE + CORNER) * side
+        for j, start, wide_start in ((0, Y0 - CORNER, Y0 - 8), (1, Y0 + SIDE, Y0 + SIDE)):
+            rows, more = CORNER * CORNER, 16 if step == 0 else 0
+            ref = recv_c.at[step, 2 * side + j]
+            arrive(step, 2 * side + j, ref, rows + more)
+            stage[j] = ref[0:rows, :].astype(F32)
+            for i in range(CORNER):
+                field[x_from + i, start : start + CORNER, :] = stage[j, CORNER * i : CORNER * (i + 1), :]
+            if step == 0:
+                unpack_winds(ref[rows : rows + more, :], winds_from, slice(wide_start, wide_start + 8))
 
     pack(0)
     pl.semaphore_wait(barrier, len(neighbours) + len(partners))
@@ -276,13 +299,17 @@
         for j in range(3):
             weights[j][i].start()
 
-    regimes = regime_in[...]
-    member = jnp.where(regimes == iota((8, 256), 0), 1.0, 0.0)
+    row_of = iota((1, 256), 1) // SIDE
+    late = jnp.where((row_of >= late_from) & (row_of < late_from + LATE), 1, 0)
+    groups = regime_in[...] + REGIMES * late
+    member = jnp.where(groups == iota((8, 256), 0), 1.0, 0.0)
     earlier = jnp.where(iota((256, 256), 0) < iota((256, 256), 1), 1.0, 0.0).astype(BF16)
     place = member * dot(member.astype(BF16), earlier)
     tiles = jnp.floor((jnp.sum(member, axis=1, keepdims=True) + (TILE - 1)) * (1.0 / TILE))
-    before = jnp.where(iota((8, 8), 1) < iota((8, 8), 0), 1.0, 0.0).astype(BF16)
+    one, other = iota((8, 8), 0), iota((8, 8), 1)
+    before = jnp.where((other < one) & (other // REGIMES == one // REGIMES), 1.0, 0.0).astype(BF16)
     starts = dot(before, jnp.broadcast_to(tiles, (8, LANES)).astype(BF16))[:, 0:1]
+    starts = starts + jnp.where(iota((8, 1), 0) >= REGIMES, float(SAFE_TILES), 0.0)
     start = member * starts
     slot_row = jnp.sum(place + TILE * start, axis=0, keepdims=True)
     same = jnp.where(iota((256, 256), 0) == iota((256, 256), 1), 1.0, 0.0).astype(BF16)
@@ -298,12 +325,16 @@
         slot_row == iota((SLOTS, 256), 0).astype(F32), 1.0, 0.0
     ).astype(BF16)
     answers[SLOTS:, :] = jnp.zeros((PAD_SLOTS - SLOTS, LANES), BF16)
-    tile_regimes = [0] * TILES
-    used = 0
-    for r in range(REGIMES - 1):
-        named = jnp.sum(jnp.where(regimes == r, 1, 0))
-        used = used + (named + (TILE - 1)) // TILE
-        tile_regimes = [r_of + jnp.where(t >= used, 1, 0) for t, r_of in enumerate(tile_regimes)]
+    dyn[...] = jnp.zeros((SIDE * SIDE, LANES), F32)
+    tile_regimes = []
+    for part, count in enumerate((SAFE_TILES, LATE_TILES)):
+        numbers = [0] * count
+        used = 0
+        for r in range(REGIMES - 1):
+            named = jnp.sum(jnp.where(groups == REGIMES * part + r, 1, 0))
+            used = used + (named + (TILE - 1)) // TILE
+            numbers = [number + jnp.where(t >= used, 1, 0) for t, number in enumerate(numbers)]
+        tile_regimes += numbers
 
     level_of = iota((TILE, LANES), 1) % LEVELS
     square = jnp.zeros((LANES, LANES), BF16)
@@ -367,44 +398,70 @@
             answer = jnp.where(level_of == m, pieces[m], answer)
         return answer.astype(BF16)
 
-    def network(first_time):
-        tiles = [lifted(t) for t in range(TILES)]
+    def network(numbers, first_time):
+        tiles = [lifted(t) for t in numbers]
         for layer in range(LAYERS):
             if first_time:
                 for j in range(3):
                     weights[j][1 + layer].wait_recv()
-            tiles = [layered(t, layer, tiles[t]) for t in range(TILES)]
-        results = [answered(t, tiles[t]) for t in range(TILES)]
-        for t in range(TILES):
-            answers[t * TILE : (t + 1) * TILE, :] = results[t]
-
-    own = (slice(X0, X0 + SIDE), slice(Y0, Y0 + SIDE), slice(None))
+            tiles = [layered(t, layer, halves) for t, halves in zip(numbers, tiles)]
+        results = [answered(t, halves) for t, halves in zip(numbers, tiles)]
+        for t, result in zip(numbers, results):
+            answers[t * TILE : (t + 1) * TILE, :] = result
+
+    def advance(x_from, rows, safe):
+        more = 2 * (4 if safe else 0)
+        ys = slice(Y0 - 4, Y0 + SIDE + 4)
+        at = X0 - 4 + x_from if safe else X0 - 4 + (SAFE + 8) * upper
+        xs = pl.ds(at, rows + more)
+        first[xs, ys, :] = field[xs, ys, :] + (1.0 / 6.0) * local_tendency(
+            field, east, north, flux, at, rows + more, ys
+        )
+        more = 2 * (2 if safe else 0)
+        ys = slice(Y0 - 2, Y0 + SIDE + 2)
+        at = X0 - 2 + x_from if safe else X0 - 2 + (SAFE + 4) * upper
+        xs = pl.ds(at, rows + more)
+        second[xs, ys, :] = (
+            0.75 * field[xs, ys, :]
+            + 0.25 * first[xs, ys, :]
+            + (0.25 / 6.0) * local_tendency(first, east, north, flux, at, rows + more, ys)
+        )
+        ys = slice(Y0, Y0 + SIDE)
+        at = X0 + x_from
+        xs = pl.ds(at, rows)
+        value = (
+            (1.0 / 3.0) * field[xs, ys, :]
+            + (2.0 / 3.0) * second[xs, ys, :]
+            + (1.0 / 9.0) * local_tendency(second, east, north, flux, at, rows, ys)
+        )
+        cells = pl.ds(pl.multiple_of(x_from * SIDE, SIDE), rows * SIDE)
+        dyn[cells, :] = value.reshape(rows * SIDE, LANES)
+
+    def half_step(step, safe):
+        x_from, rows = (safe_from, SAFE) if safe else (late_from, LATE)
+        numbers = range(SAFE_TILES) if safe else range(SAFE_TILES, TILES)
+        slots = slice(0, SAFE_SLOTS) if safe else slice(SAFE_SLOTS, SLOTS)
+        read = slice(0, SAFE_SLOTS) if safe else slice(SAFE_SLOTS, PAD_SLOTS)
+        advance(x_from, rows, safe)
+        ordered[slots, :] = dot(pick[slots, :], dyn[...].astype(BF16)).astype(BF16)
+        network(numbers, safe and step == 0)
+        cells = pl.ds(pl.multiple_of(x_from * SIDE, SIDE), rows * SIDE)
+        final = dyn[cells, :] + dot(unpick[cells, read], answers[read, :])
+        if step < STEPS - 1:
+            xs = pl.ds(X0 + x_from, rows)
+            field[xs, Y0 : Y0 + SIDE, :] = final.reshape(rows, SIDE, LANES)
+        else:
+            for i in range(rows):
+                out_ref[pl.ds(x_from + i, LANES, stride=SIDE), :] = final[SIDE * i : SIDE * (i + 1)].T
+
     for step in range(STEPS):
         if step:
             pack(step)
             halo = [halo_copy(step, k) for k in range(8)]
             for copy in halo:
                 copy.start()
-        for copy in halo:
-            copy.wait_recv()
-        unpack(step)
-        xs, ys = slice(X0 - 4, X0 + SIDE + 4), slice(Y0 - 4, Y0 + SIDE + 4)
-        first[xs, ys, :] = field[xs, ys, :] + (1.0 / 6.0) * local_tendency(
-            field, east, north, flux, xs, ys
-        )
-        xs, ys = slice(X0 - 2, X0 + SIDE + 2), slice(Y0 - 2, Y0 + SIDE + 2)
-        second[xs, ys, :] = (
-            0.75 * field[xs, ys, :]
-            + 0.25 * first[xs, ys, :]
-            + (0.25 / 6.0) * local_tendency(first, east, north, flux, xs, ys)
-        )
-        xs, ys = own[0], own[1]
-        dyn = (
-            (1.0 / 3.0) * field[own]
-            + (2.0 / 3.0) * second[own]
-            + (1.0 / 9.0) * local_tendency(second, east, north, flux, xs, ys)
-        ).reshape(SIDE * SIDE, LANES)
-        ordered[...] = dot(pick[...], dyn.astype(BF16)).astype(BF16)
+        receive_y(step)
+        receive_x(step, 1 - upper)
         if step == 0:
             for j in range(3):
                 weights[j][0].wait_recv()
@@ -414,12 +471,9 @@
             for r in range(REGIMES):
                 lift_map[r] = dot(to_lift, small[r]).astype(BF16)
                 out_map[r] = dot(to_out, small[r]).astype(BF16)
-        network(step == 0)
-        final = dyn + dot(unpick[...], answers[...])
-        if step == STEPS - 1:
-            out_ref[...] = final
-        else:
-            field[own] = final.reshape(SIDE, SIDE, LANES)
+        half_step(step, True)
+        receive_x(step, upper)
+        half_step(step, False)
         for copy in halo:
             copy.wait_send()
     for j in range(3):
@@ -433,7 +487,7 @@
     dma = pltpu.SemaphoreType.DMA
     result = pl.pallas_call(
         kernel,
-        out_shape=jax.ShapeDtypeStruct((cells, LANES), F32),
+        out_shape=jax.ShapeDtypeStruct((LANES * SIDE, SIDE), F32),
         in_specs=[pl.BlockSpec(memory_space=pl.ANY)] * 6,
         out_specs=pl.BlockSpec(memory_space=pltpu.VMEM),
         scratch_shapes=[
@@ -461,6 +515,7 @@
             pltpu.VMEM((cells, PAD_SLOTS), BF16),
             pltpu.VMEM((SLOTS, LANES), BF16),
             pltpu.VMEM((PAD_SLOTS, LANES), BF16),
+            pltpu.VMEM((cells, LANES), F32),
             dma((6,)),
             dma((STEPS, 8)), dma((STEPS, 8)),
             dma((3, LAYERS)), dma((3, LAYERS)),
@@ -477,7 +532,7 @@
         emu_output[0],
         emu_conv.reshape(3 * LAYERS, LANES, LANES),
     )
-    return result.reshape(SIDE, SIDE, VARS, LEVELS).transpose(2, 3, 0, 1)
+    return result.reshape(VARS, LEVELS, SIDE, SIDE)
 
 
 def solution(mesh):

time: 42.9 us -> 46.4 us (1.082)
  Pallas kernels: 40 us -> 44 us
    pallas_call x1, Pallas kernels: 40 us -> 44 us  [per_device(): pl.pallas_call(kernel, out_shape=jax.ShapeDtypeStruct((LANES * SIDE, SIDE...]
    reshape x2 -> x0, local copies, waits for them, and re-layouts: 2.71 us -> none  [per_device(): return result.reshape(SIDE, SIDE, VARS, LEVELS).transpose(2, 3, 0, 1)]
    unnamed x0 -> x1, local copies, waits for them, and re-layouts: none -> 2.27 us
where the time goes in v3:
time: 46.4 us; the launch traced here: 46.2 us
  Pallas kernels  44 us (95%)
  local copies, waits for them, and re-layouts  2.27 us (5%)
    pallas_call x1, Pallas kernels, per_device(): pl.pallas_call(kernel, out_shape=jax.ShapeDtypeStruct((LANES * SIDE, SIDE...  44 us
    unnamed x1, local copies, waits for them, and re-layouts  2.27 us

profile of v3, /device:TPU:1, one launch (start us, length us, event | category | flops | bytes accessed | tf_op | source)
XLA Modules:
  0.0 46.2 jit_solution(13396383600834375144)
XLA Ops:
  0.0 44.0 %shard_map.64 = f32[2048,16]{1,0:T(8,128)} custom-call(f32[2048,16]{1,0:T(8,128)} %bitcast.10, f32[512,16]{1,0:T(8,128)} %bitcast.12, s32[1,256]{1,0:T(1,128)} %bitcast.15, bf16[8,128]{1,0:T(8,128)(2,1)} %bitcast.13, bf16[8,128]{1,0:T(8,128)(2,1)} %bitcast.14, bf16[12,128,128]{2,1,0:T(8,128)(2,1)} %bitcast.11), custom_call_target="tpu_custom_call" | custom-call | tf_op jit(solution)/shard_map/pallas_call | solution.py:488
  44.0 2.3 %copy.8 = f32[8,16,16,16]{3,2,1,0:T(8,128)} copy(f32[8,16,16,16]{3,2,1,0:T(8,128)} %bitcast.9) | data formatting | bytes 262144

commit v4 on v3

--- a/solution.py
+++ b/solution.py
@@ -18,11 +18,9 @@
 TILE = 32
 LATE = 6
 SAFE = SIDE - LATE
-SAFE_TILES, LATE_TILES = 8, 6
-TILES = SAFE_TILES + LATE_TILES
-SAFE_SLOTS = SAFE_TILES * TILE
+TILES = 11
 SLOTS = TILES * TILE
-PAD_SLOTS = 512
+PAD_SLOTS = 384
 CORNER = 4
 X0, Y0 = 8, 8
 PAD_X, PAD_Y = 32, 32
@@ -299,17 +297,13 @@
         for j in range(3):
             weights[j][i].start()
 
-    row_of = iota((1, 256), 1) // SIDE
-    late = jnp.where((row_of >= late_from) & (row_of < late_from + LATE), 1, 0)
-    groups = regime_in[...] + REGIMES * late
-    member = jnp.where(groups == iota((8, 256), 0), 1.0, 0.0)
+    regimes = regime_in[...]
+    member = jnp.where(regimes == iota((8, 256), 0), 1.0, 0.0)
     earlier = jnp.where(iota((256, 256), 0) < iota((256, 256), 1), 1.0, 0.0).astype(BF16)
     place = member * dot(member.astype(BF16), earlier)
     tiles = jnp.floor((jnp.sum(member, axis=1, keepdims=True) + (TILE - 1)) * (1.0 / TILE))
-    one, other = iota((8, 8), 0), iota((8, 8), 1)
-    before = jnp.where((other < one) & (other // REGIMES == one // REGIMES), 1.0, 0.0).astype(BF16)
+    before = jnp.where(iota((8, 8), 1) < iota((8, 8), 0), 1.0, 0.0).astype(BF16)
     starts = dot(before, jnp.broadcast_to(tiles, (8, LANES)).astype(BF16))[:, 0:1]
-    starts = starts + jnp.where(iota((8, 1), 0) >= REGIMES, float(SAFE_TILES), 0.0)
     start = member * starts
     slot_row = jnp.sum(place + TILE * start, axis=0, keepdims=True)
     same = jnp.where(iota((256, 256), 0) == iota((256, 256), 1), 1.0, 0.0).astype(BF16)
@@ -325,16 +319,12 @@
         slot_row == iota((SLOTS, 256), 0).astype(F32), 1.0, 0.0
     ).astype(BF16)
     answers[SLOTS:, :] = jnp.zeros((PAD_SLOTS - SLOTS, LANES), BF16)
-    dyn[...] = jnp.zeros((SIDE * SIDE, LANES), F32)
-    tile_regimes = []
-    for part, count in enumerate((SAFE_TILES, LATE_TILES)):
-        numbers = [0] * count
-        used = 0
-        for r in range(REGIMES - 1):
-            named = jnp.sum(jnp.where(groups == REGIMES * part + r, 1, 0))
-            used = used + (named + (TILE - 1)) // TILE
-            numbers = [number + jnp.where(t >= used, 1, 0) for t, number in enumerate(numbers)]
-        tile_regimes += numbers
+    tile_regimes = [0] * TILES
+    used = 0
+    for r in range(REGIMES - 1):
+        named = jnp.sum(jnp.where(regimes == r, 1, 0))
+        used = used + (named + (TILE - 1)) // TILE
+        tile_regimes = [number + jnp.where(t >= used, 1, 0) for t, number in enumerate(tile_regimes)]
 
     level_of = iota((TILE, LANES), 1) % LEVELS
     square = jnp.zeros((LANES, LANES), BF16)
@@ -398,16 +388,16 @@
             answer = jnp.where(level_of == m, pieces[m], answer)
         return answer.astype(BF16)
 
-    def network(numbers, first_time):
-        tiles = [lifted(t) for t in numbers]
+    def network(first_time):
+        tiles = [lifted(t) for t in range(TILES)]
         for layer in range(LAYERS):
             if first_time:
                 for j in range(3):
                     weights[j][1 + layer].wait_recv()
-            tiles = [layered(t, layer, halves) for t, halves in zip(numbers, tiles)]
-        results = [answered(t, halves) for t, halves in zip(numbers, tiles)]
-        for t, result in zip(numbers, results):
-            answers[t * TILE : (t + 1) * TILE, :] = result
+            tiles = [layered(t, layer, tiles[t]) for t in range(TILES)]
+        results = [answered(t, tiles[t]) for t in range(TILES)]
+        for t in range(TILES):
+            answers[t * TILE : (t + 1) * TILE, :] = results[t]
 
     def advance(x_from, rows, safe):
         more = 2 * (4 if safe else 0)
@@ -437,23 +427,6 @@
         cells = pl.ds(pl.multiple_of(x_from * SIDE, SIDE), rows * SIDE)
         dyn[cells, :] = value.reshape(rows * SIDE, LANES)
 
-    def half_step(step, safe):
-        x_from, rows = (safe_from, SAFE) if safe else (late_from, LATE)
-        numbers = range(SAFE_TILES) if safe else range(SAFE_TILES, TILES)
-        slots = slice(0, SAFE_SLOTS) if safe else slice(SAFE_SLOTS, SLOTS)
-        read = slice(0, SAFE_SLOTS) if safe else slice(SAFE_SLOTS, PAD_SLOTS)
-        advance(x_from, rows, safe)
-        ordered[slots, :] = dot(pick[slots, :], dyn[...].astype(BF16)).astype(BF16)
-        network(numbers, safe and step == 0)
-        cells = pl.ds(pl.multiple_of(x_from * SIDE, SIDE), rows * SIDE)
-        final = dyn[cells, :] + dot(unpick[cells, read], answers[read, :])
-        if step < STEPS - 1:
-            xs = pl.ds(X0 + x_from, rows)
-            field[xs, Y0 : Y0 + SIDE, :] = final.reshape(rows, SIDE, LANES)
-        else:
-            for i in range(rows):
-                out_ref[pl.ds(x_from + i, LANES, stride=SIDE), :] = final[SIDE * i : SIDE * (i + 1)].T
-
     for step in range(STEPS):
         if step:
             pack(step)
@@ -462,6 +435,7 @@
                 copy.start()
         receive_y(step)
         receive_x(step, 1 - upper)
+        advance(safe_from, SAFE, True)
         if step == 0:
             for j in range(3):
                 weights[j][0].wait_recv()
@@ -471,9 +445,15 @@
             for r in range(REGIMES):
                 lift_map[r] = dot(to_lift, small[r]).astype(BF16)
                 out_map[r] = dot(to_out, small[r]).astype(BF16)
-        half_step(step, True)
         receive_x(step, upper)
-        half_step(step, False)
+        advance(late_from, LATE, False)
+        ordered[...] = dot(pick[...], dyn[...].astype(BF16)).astype(BF16)
+        network(step == 0)
+        final = dyn[...] + dot(unpick[...], answers[...])
+        if step < STEPS - 1:
+            field[X0 : X0 + SIDE, Y0 : Y0 + SIDE, :] = final.reshape(SIDE, SIDE, LANES)
+        else:
+            out_ref[...] = final
         for copy in halo:
             copy.wait_send()
     for j in range(3):
@@ -487,8 +467,8 @@
     dma = pltpu.SemaphoreType.DMA
     result = pl.pallas_call(
         kernel,
-        out_shape=jax.ShapeDtypeStruct((LANES * SIDE, SIDE), F32),
-        in_specs=[pl.BlockSpec(memory_space=pl.ANY)] * 6,
+        out_shape=jax.ShapeDtypeStruct((cells, LANES), F32),
+        in_specs=[pl.BlockSpec(memory_space=pltpu.HBM)] * 6,
         out_specs=pl.BlockSpec(memory_space=pltpu.VMEM),
         scratch_shapes=[
             pltpu.VMEM((LANES * SIDE, SIDE), F32),
@@ -522,17 +502,22 @@
             dma((3,)), dma((3,)),
         ],
         compiler_params=pltpu.CompilerParams(
-            collective_id=0, has_side_effects=True, vmem_limit_bytes=60 * 2**20
+            collective_id=0, has_side_effects=True, vmem_limit_bytes=32 * 2**20
         ),
     )(
-        state.reshape(LANES * SIDE, SIDE),
-        winds.reshape(2 * LEVELS * SIDE, SIDE),
-        regime_table.reshape(1, cells),
-        emu_lift[0].T,
-        emu_output[0],
-        emu_conv.reshape(3 * LAYERS, LANES, LANES),
-    )
-    return result.reshape(VARS, LEVELS, SIDE, SIDE)
+        *[
+            pltpu.with_memory_space_constraint(operand, pltpu.HBM)
+            for operand in (
+                state.reshape(LANES * SIDE, SIDE),
+                winds.reshape(2 * LEVELS * SIDE, SIDE),
+                regime_table.reshape(1, cells),
+                emu_lift[0].T,
+                emu_output[0],
+                emu_conv.reshape(3 * LAYERS, LANES, LANES),
+            )
+        ]
+    )
+    return result.reshape(SIDE, SIDE, VARS, LEVELS).transpose(2, 3, 0, 1)
 
 
 def solution(mesh):

time: 46.4 us -> 40 us (0.86)
  Pallas kernels: 44 us -> 38 us
  local copies, waits for them, and re-layouts: 2.27 us -> 1.8 us
    pallas_call x1, Pallas kernels: 44 us -> 38 us  [per_device(): pl.pallas_call(kernel, out_shape=jax.ShapeDtypeStruct((cells, LANES), F32...]
    unnamed x1 -> x0, local copies, waits for them, and re-layouts: 2.27 us -> none
    reshape x0 -> x2, local copies, waits for them, and re-layouts: none -> 1.8 us  [per_device(): return result.reshape(SIDE, SIDE, VARS, LEVELS).transpose(2, 3, 0, 1)]
where the time goes in v4:
time: 40 us; the launch traced here: 39.8 us
  Pallas kernels  38 us (95%)
  local copies, waits for them, and re-layouts  1.8 us (4%)
    pallas_call x1, Pallas kernels, per_device(): pl.pallas_call(kernel, out_shape=jax.ShapeDtypeStruct((cells, LANES), F32...  38 us
    reshape x2, local copies, waits for them, and re-layouts, per_device(): return result.reshape(SIDE, SIDE, VARS, LEVELS).transpose(2, 3, 0, 1)  1.8 us

profile of v4, /device:TPU:1, one launch (start us, length us, event | category | flops | bytes accessed | tf_op | source)
XLA Modules:
  0.0 39.8 jit_solution(14168522583711390564)
XLA Ops:
  0.0 38.0 %shard_map.64 = f32[256,128]{1,0:T(8,128)S(1)} custom-call(f32[2048,16]{1,0:T(8,128)} %bitcast.9, f32[512,16]{1,0:T(8,128)} %bitcast.11, s32[1,256]{1,0:T(1,128)} %bitcast.14, bf16[8,128]{1,0:T(8,128)(2,1)} %bitcast.12, bf16[8,128]{1,0:T(8,128)(2,1)} %bitcast.13, bf16[12,128,128]{2,1,0:T(8,128)(2,1)} %bitcast.10), custom_call_target="tpu_custom_call" | custom-call | tf_op jit(solution)/shard_map/pallas_call | solution.py:468
  38.0 0.3 reshape.19
  38.4 1.5 %copy.7 = f32[16,16,8,16]{1,0,3,2:T(8,128)} copy(f32[16,16,8,16]{3,2,1,0:T(8,128)S(1)} %reshape.19) | data formatting | bytes 262144 | tf_op jit(solution)/shard_map/reshape | solution.py:520

commit v5 on v4

--- a/solution.py
+++ b/solution.py
@@ -119,7 +119,7 @@
     partners = (
         (tile, chip * 2 + (1 - core), emu),
         (tile, (1 - chip) * 2 + core, emu),
-        (far_tile, (1 - chip) * 2 + (1 - core), emu),
+        (far_tile, (1 - chip) * 2 + core, emu),
     )
     neighbours = [neighbour(dx, dy) for dx, dy in DIRECTIONS]
 
@@ -186,7 +186,7 @@
             device_id_type=MESH,
         )
 
-    def pack(step):
+    def pack(step, then=lambda k: None):
         for k, (dx, dy) in enumerate(DIRECTIONS):
             sent, _ = buffers(step, k)
             xs, ys = sent_box(dx, dy)
@@ -206,6 +206,7 @@
                         piece = winds[gx, gy, :].reshape(more, LANES)
                         packed = jnp.where(quarter == c * 4 + g, piece, packed)
                 sent[rows : rows + more, :] = packed.astype(BF16)
+            then(k)
 
     def arrive(step, k, ref, rows):
         pltpu.make_async_remote_copy(
@@ -268,34 +269,44 @@
         conv[layer][sect] = 0.5 * taps_in[3 * layer : 3 * layer + 3]
     small[sect] = jnp.concatenate([lift_in[...], output_in[...]], axis=0)
 
-    def weight_copies(j):
-        copies = [
-            pltpu.make_async_remote_copy(
-                src_ref=small.at[sect],
-                dst_ref=small.at[sect],
-                send_sem=small_send.at[j],
-                recv_sem=small_recv.at[j],
-                device_id=partners[j],
-                device_id_type=MESH,
-            )
-        ]
-        for layer in range(LAYERS):
-            copies.append(
-                pltpu.make_async_remote_copy(
-                    src_ref=conv[layer].at[sect],
-                    dst_ref=conv[layer].at[sect],
-                    send_sem=weight_send.at[j, layer],
-                    recv_sem=weight_recv.at[j, layer],
-                    device_id=partners[j],
-                    device_id_type=MESH,
-                )
-            )
-        return copies
-
-    weights = [weight_copies(j) for j in range(3)]
-    for i in range(LAYERS + 1):
-        for j in range(3):
-            weights[j][i].start()
+    other = (1 - chip) * 2 + core
+
+    def taps_copy(j, layer, regime, handed=0):
+        return pltpu.make_async_remote_copy(
+            src_ref=conv[layer].at[regime],
+            dst_ref=conv[layer].at[regime],
+            send_sem=weight_send.at[handed, j, layer],
+            recv_sem=weight_recv.at[handed, j, layer],
+            device_id=partners[j],
+            device_id_type=MESH,
+        )
+
+    def small_copy(j, regime, handed=0):
+        return pltpu.make_async_remote_copy(
+            src_ref=small.at[regime],
+            dst_ref=small.at[regime],
+            send_sem=small_send.at[handed, j],
+            recv_sem=small_recv.at[handed, j],
+            device_id=partners[j],
+            device_id_type=MESH,
+        )
+
+    route = (1, 2, 1, 2)
+    own_small = [small_copy(0, sect), small_copy(1, sect)]
+    own_taps = [taps_copy(route[layer], layer, sect) for layer in range(LAYERS)]
+    core_taps = [taps_copy(0, layer, sect) for layer in range(LAYERS)]
+    handed_small = [small_copy(0, other, 1)]
+    handed_taps = [taps_copy(0, layer, other, 1) for layer in range(LAYERS)]
+    for copy in own_small + own_taps + core_taps:
+        copy.start()
+    outgoing = own_small + own_taps + core_taps + handed_small + handed_taps
+
+    def hand_on(*layers):
+        for layer in layers:
+            taps_copy(route[layer], layer, other).wait_recv()
+            handed_taps[layer].start()
+
+    arriving = [(core_taps[layer], handed_taps[layer]) for layer in range(LAYERS)]
 
     regimes = regime_in[...]
     member = jnp.where(regimes == iota((8, 256), 0), 1.0, 0.0)
@@ -392,9 +403,11 @@
         tiles = [lifted(t) for t in range(TILES)]
         for layer in range(LAYERS):
             if first_time:
-                for j in range(3):
-                    weights[j][1 + layer].wait_recv()
+                for copy in arriving[layer]:
+                    copy.wait_recv()
             tiles = [layered(t, layer, tiles[t]) for t in range(TILES)]
+            if first_time and layer == 0:
+                hand_on(2, 3)
         results = [answered(t, tiles[t]) for t in range(TILES)]
         for t in range(TILES):
             answers[t * TILE : (t + 1) * TILE, :] = results[t]
@@ -429,16 +442,18 @@
 
     for step in range(STEPS):
         if step:
-            pack(step)
             halo = [halo_copy(step, k) for k in range(8)]
-            for copy in halo:
-                copy.start()
+            pack(step, lambda k: halo[k].start())
         receive_y(step)
+        if step == 0:
+            small_copy(1, other).wait_recv()
+            handed_small[0].start()
         receive_x(step, 1 - upper)
         advance(safe_from, SAFE, True)
         if step == 0:
-            for j in range(3):
-                weights[j][0].wait_recv()
+            hand_on(0, 1)
+            own_small[0].wait_recv()
+            handed_small[0].wait_recv()
             row, column = iota((LANES, 16), 0), iota((LANES, 16), 1)
             to_lift = jnp.where(row // LEVELS == column, 0.5, 0.0).astype(BF16)
             to_out = jnp.where(row // LEVELS + VARS == column, 2.0, 0.0).astype(BF16)
@@ -453,12 +468,12 @@
         if step < STEPS - 1:
             field[X0 : X0 + SIDE, Y0 : Y0 + SIDE, :] = final.reshape(SIDE, SIDE, LANES)
         else:
-            out_ref[...] = final
+            for x in range(SIDE):
+                out_ref[pl.ds(x, LANES, stride=SIDE), :] = final[SIDE * x : SIDE * (x + 1)].T
         for copy in halo:
             copy.wait_send()
-    for j in range(3):
-        for copy in weights[j]:
-            copy.wait_send()
+    for copy in outgoing:
+        copy.wait_send()
 
 
 def per_device(state, winds, regime_table, emu_lift, emu_conv, emu_output):
@@ -467,7 +482,7 @@
     dma = pltpu.SemaphoreType.DMA
     result = pl.pallas_call(
         kernel,
-        out_shape=jax.ShapeDtypeStruct((cells, LANES), F32),
+        out_shape=jax.ShapeDtypeStruct((LANES * SIDE, SIDE), F32),
         in_specs=[pl.BlockSpec(memory_space=pltpu.HBM)] * 6,
         out_specs=pl.BlockSpec(memory_space=pltpu.VMEM),
         scratch_shapes=[
@@ -498,8 +513,8 @@
             pltpu.VMEM((cells, LANES), F32),
             dma((6,)),
             dma((STEPS, 8)), dma((STEPS, 8)),
-            dma((3, LAYERS)), dma((3, LAYERS)),
-            dma((3,)), dma((3,)),
+            dma((2, 3, LAYERS)), dma((2, 3, LAYERS)),
+            dma((2, 3)), dma((2, 3)),
         ],
         compiler_params=pltpu.CompilerParams(
             collective_id=0, has_side_effects=True, vmem_limit_bytes=32 * 2**20
@@ -517,7 +532,7 @@
             )
         ]
     )
-    return result.reshape(SIDE, SIDE, VARS, LEVELS).transpose(2, 3, 0, 1)
+    return result.reshape(VARS, LEVELS, SIDE, SIDE)
 
 
 def solution(mesh):

time: 40 us -> 39.4 us (0.985)
  local copies, waits for them, and re-layouts: 1.8 us -> 0.97 us
    reshape x2 -> x0, local copies, waits for them, and re-layouts: 1.8 us -> none  [per_device(): return result.reshape(SIDE, SIDE, VARS, LEVELS).transpose(2, 3, 0, 1)]
    unnamed x0 -> x1, local copies, waits for them, and re-layouts: none -> 0.97 us
where the time goes in v5:
time: 39.4 us; the launch traced here: 39.3 us
  Pallas kernels  38.3 us (97%)
  local copies, waits for them, and re-layouts  0.97 us (2%)
    pallas_call x1, Pallas kernels, per_device(): pl.pallas_call(kernel, out_shape=jax.ShapeDtypeStruct((LANES * SIDE, SIDE...  38.3 us
    unnamed x1, local copies, waits for them, and re-layouts  0.97 us

profile of v5, /device:TPU:1, one launch (start us, length us, event | category | flops | bytes accessed | tf_op | source)
XLA Modules:
  0.0 39.3 jit_solution(7139390965453573557)
XLA Ops:
  0.0 38.3 %shard_map.64 = f32[2048,16]{1,0:T(8,128)S(1)} custom-call(f32[2048,16]{1,0:T(8,128)} %bitcast.10, f32[512,16]{1,0:T(8,128)} %bitcast.12, s32[1,256]{1,0:T(1,128)} %bitcast.15, bf16[8,128]{1,0:T(8,128)(2,1)} %bitcast.13, bf16[8,128]{1,0:T(8,128)(2,1)} %bitcast.14, bf16[12,128,128]{2,1,0:T(8,128)(2,1)} %bitcast.11), custom_call_target="tpu_custom_call" | custom-call | tf_op jit(solution)/shard_map/pallas_call | solution.py:483
  38.3 1.0 %copy.8 = f32[8,16,16,16]{3,2,1,0:T(8,128)} copy(f32[8,16,16,16]{3,2,1,0:T(8,128)S(1)} %bitcast.9) | data formatting | bytes 262144

commit v6 on v5

--- a/solution.py
+++ b/solution.py
@@ -23,7 +23,7 @@
 PAD_SLOTS = 384
 CORNER = 4
 X0, Y0 = 8, 8
-PAD_X, PAD_Y = 32, 32
+PAD_X, PAD_Y = 32, 40
 DIRECTIONS = ((1, 1), (1, -1), (-1, 1), (-1, -1), (1, 0), (-1, 0), (0, 1), (0, -1))
 BF16 = jnp.bfloat16
 F32 = jnp.float32
@@ -194,7 +194,7 @@
             if dx and dy:
                 for i in range(CORNER):
                     stage[k, CORNER * i : CORNER * (i + 1), :] = field[xs.start + i, ys, :]
-                sent[0:rows, :] = stage[k].astype(BF16)
+                sent[0:rows, :] = stage[k, 0:rows, :].astype(BF16)
             else:
                 sent[0:rows, :] = field[xs, ys, :].reshape(rows, LANES).astype(BF16)
             if step == 0:
@@ -251,7 +251,7 @@
             rows, more = CORNER * CORNER, 16 if step == 0 else 0
             ref = recv_c.at[step, 2 * side + j]
             arrive(step, 2 * side + j, ref, rows + more)
-            stage[j] = ref[0:rows, :].astype(F32)
+            stage[j, 0:rows, :] = ref[0:rows, :].astype(F32)
             for i in range(CORNER):
                 field[x_from + i, start : start + CORNER, :] = stage[j, CORNER * i : CORNER * (i + 1), :]
             if step == 0:
@@ -494,7 +494,7 @@
             pltpu.VMEM((3 * LAYERS, LANES, LANES), BF16),
             padded, padded, padded, padded, padded,
             pltpu.VMEM((24, PAD_Y, LANES), F32),
-            pltpu.VMEM((4, CORNER * CORNER, LANES), F32),
+            pltpu.VMEM((4, CORNER * CORNER + 8, LANES), F32),
             pltpu.VMEM((STEPS, 2, 128, LANES), BF16),
             pltpu.VMEM((STEPS, 2, 128, LANES), BF16),
             pltpu.VMEM((STEPS, 2, 160, LANES), BF16),

time: 39.4 us -> 39.4 us (level)
  no operation moved by 1% of the time
where the time goes in v6:
time: 39.4 us; the launch traced here: 39.3 us
  Pallas kernels  38.3 us (97%)
  local copies, waits for them, and re-layouts  0.97 us (2%)
    pallas_call x1, Pallas kernels, per_device(): pl.pallas_call(kernel, out_shape=jax.ShapeDtypeStruct((LANES * SIDE, SIDE...  38.3 us
    unnamed x1, local copies, waits for them, and re-layouts  0.97 us

profile of v6, /device:TPU:1, one launch (start us, length us, event | category | flops | bytes accessed | tf_op | source)
XLA Modules:
  0.0 39.3 jit_solution(3515304466185754248)
XLA Ops:
  0.0 38.3 %shard_map.64 = f32[2048,16]{1,0:T(8,128)S(1)} custom-call(f32[2048,16]{1,0:T(8,128)} %bitcast.10, f32[512,16]{1,0:T(8,128)} %bitcast.12, s32[1,256]{1,0:T(1,128)} %bitcast.15, bf16[8,128]{1,0:T(8,128)(2,1)} %bitcast.13, bf16[8,128]{1,0:T(8,128)(2,1)} %bitcast.14, bf16[12,128,128]{2,1,0:T(8,128)(2,1)} %bitcast.11), custom_call_target="tpu_custom_call" | custom-call | tf_op jit(solution)/shard_map/pallas_call | solution.py:483
  38.3 1.0 %copy.8 = f32[8,16,16,16]{3,2,1,0:T(8,128)} copy(f32[8,16,16,16]{3,2,1,0:T(8,128)S(1)} %bitcast.9) | data formatting | bytes 262144
